TPU v7x, 32 devices: a whole 2x2x4 slice. The times are simulated.
32 devices in a mesh: narrow: 4 (over x, core), wide: 8 (over z, y).
Axes of the slice: x: 2, y: 2, z: 4, core: 2. Of those that a mesh axis runs over, the one named last changes fastest.
Arguments:
- tokens: bfloat16 [12288, 512], P(('narrow', 'wide')), may hold values from -6 to 6
- gain_one: float32 [512], replicated, may hold values from 0.5 to 1.5
- shift_one: float32 [512], replicated, may hold values from -1.25 to 1.25
- query_w: bfloat16 [512, 512], replicated, may hold values from -0.25 to 0.25
- key_w: bfloat16 [512, 512], replicated, may hold values from -0.25 to 0.25
- value_w: bfloat16 [512, 512], replicated, may hold values from -0.25 to 0.25
- out_w: bfloat16 [512, 512], replicated, may hold values from -1.5 to 1.5
- gain_two: float32 [512], replicated, may hold values from 0.5 to 1.5
- shift_two: float32 [512], replicated, may hold values from -1.25 to 1.25
- router_w: bfloat16 [512, 8], replicated, may hold values from -0.1875 to 0.1875
- up_w: bfloat16 [8, 512, 2048], P('wide'), may hold values from -0.25 to 0.25
- up_bias: float32 [8, 2048], P('wide'), may hold values from -0.625 to 0.625
- down_w: bfloat16 [8, 2048, 512], P('wide'), may hold values from -4 to 4
- down_bias: float32 [8, 512], P('wide'), may hold values from -12 to 12
- picks: int32 [12288, 2], P(('narrow', 'wide')), may hold values from 0 to 7, all different within a row
- ranks: int32 [12288, 2], P(('narrow', 'wide')), may hold values from 0 to 767, as said below
- out_grad: bfloat16 [12288, 512], P(('narrow', 'wide')), may hold values from -6 to 6
Outputs:
- block_out: bfloat16 [12288, 512], P(('narrow', 'wide'))
- tokens_grad: bfloat16 [12288, 512], P(('narrow', 'wide'))
- gain_one_grad: float32 [512], replicated
- shift_one_grad: float32 [512], replicated
- query_grad: float32 [512, 512], replicated
- key_grad: float32 [512, 512], replicated
- value_grad: float32 [512, 512], replicated
- out_w_grad: float32 [512, 512], replicated
- gain_two_grad: float32 [512], replicated
- shift_two_grad: float32 [512], replicated
- router_grad: float32 [512, 8], replicated
- up_grad: float32 [8, 512, 2048], P('wide')
- up_bias_grad: float32 [8, 2048], P('wide')
- down_grad: float32 [8, 2048, 512], P('wide')
- down_bias_grad: float32 [8, 512], P('wide')
- expert_counts: int32 [8, 2], replicated
Inputs may be any that keep to these rules, and one draw needn't show every extreme that they name: `picks`: the two experts of a row differ. `ranks`: within the 384 tokens of each device block, the 768 entries are all different; a smaller rank takes its slot first.
All inputs are finite; a program needn't handle non-finite values.
Results may differ from a plain program's by a relative error of at most 0.017.
Values may be sent and summed in bfloat16 or wider, within the bound.
No kernel may reach another device: no remote copies, remote signals or barrier semaphores. Data moves between devices by JAX's collectives and lax.ppermute only.
A program may use at most 128 MiB of HBM per device.

v0:
```python
import functools
import math

import jax
import jax.numpy as jnp
from jax import lax
from jax.experimental import pallas as pl
from jax.experimental.pallas import tpu as pltpu
from jax.sharding import PartitionSpec as P

HEADS = 8
PATCHES = 48
EPSILON = 1e-06
LANES = 128
MIB = 1 << 20
F32 = jnp.float32
BF16 = jnp.bfloat16

VMEM = functools.partial(pl.BlockSpec, memory_space=pltpu.VMEM)
SMEM = functools.partial(pl.BlockSpec, memory_space=pltpu.SMEM)


def shape(dims, dtype):
    return jax.ShapeDtypeStruct(dims, dtype)


def dot(a, b):
    return jnp.dot(a, b, preferred_element_type=F32)


def dot_nt(a, b):
    return lax.dot_general(a, b, (((1,), (1,)), ((), ())), preferred_element_type=F32)


def dot_tn(a, b):
    return lax.dot_general(a, b, (((0,), (0,)), ((), ())), preferred_element_type=F32)


def params(mib):
    return pltpu.CompilerParams(vmem_limit_bytes=mib * MIB)


def cost(us):
    return pl.CostEstimate(flops=int(us * 1.0e9), bytes_accessed=int(us * 1.0e6), transcendentals=0)


def norm_rows(values):
    center = values - jnp.mean(values, axis=-1, keepdims=True)
    spread = jnp.mean(center * center, axis=-1, keepdims=True)
    rate = lax.rsqrt(spread + EPSILON)
    return center * rate, rate


def norm_back(hat, rate, gain, grad):
    scaled = grad * gain
    mean_one = jnp.mean(scaled, axis=-1, keepdims=True)
    mean_two = jnp.mean(scaled * hat, axis=-1, keepdims=True)
    return rate * (scaled - mean_one - hat * mean_two)


def route_kernel(capacity, experts, picks_ref, ranks_ref, grad_ref, spread_ref, target_ref, count_ref, sent_ref):
    count = picks_ref.shape[1]
    slots_all = experts * capacity
    span = 1 << (2 * count - 1).bit_length()
    picks = picks_ref[...].astype(F32)
    base = picks * span
    order = base + ranks_ref[...].astype(F32)
    padded = jnp.concatenate([picks, order, jnp.zeros((4, count), F32)], axis=0)
    turned = jnp.transpose(padded)
    targets = []
    for j in range(2):
        row = order[j : j + 1]
        floor = base[j : j + 1]
        slot = jnp.zeros((1, count), F32)
        for other in range(2):
            column = turned[:, 2 + other : 3 + other]
            ahead = (column < row) & (column >= floor)
            slot = slot + jnp.sum(jnp.where(ahead, 1.0, 0.0), axis=0, keepdims=True)
        kept = slot < capacity
        targets.append(jnp.where(kept, picks[j : j + 1] * capacity + slot, float(slots_all)))
    target_turned = jnp.transpose(jnp.concatenate(targets + [jnp.zeros((6, count), F32)], axis=0))
    target_ref[...] = target_turned
    lane = lax.broadcasted_iota(jnp.int32, (count, LANES), 1).astype(F32)
    kept_count = jnp.zeros((1, LANES), F32)
    all_count = jnp.zeros((1, LANES), F32)
    for j in range(2):
        named = jnp.where(turned[:, j : j + 1] == lane, 1.0, 0.0)
        live = jnp.where(target_turned[:, j : j + 1] < slots_all, 1.0, 0.0)
        all_count = all_count + jnp.sum(named, axis=0, keepdims=True)
        kept_count = kept_count + jnp.sum(named * live, axis=0, keepdims=True)
    count_ref[...] = jnp.concatenate([kept_count, all_count - kept_count, jnp.zeros((6, LANES), F32)], axis=0)
    step = 64
    for start in range(0, slots_all, step):
        index = lax.broadcasted_iota(jnp.int32, (step, count), 0).astype(F32) + float(start)
        hit = (index == targets[0]) | (index == targets[1])
        spread_ref[start : start + step, :] = jnp.where(hit, 1.0, 0.0).astype(BF16)
    sent_ref[...] = dot(spread_ref[...], grad_ref[...]).astype(BF16)


def head_masks(width):
    lane = lax.broadcasted_iota(jnp.int32, (1, width), 1)
    return lane < width // 2


def stack_heads(pair, low):
    zero = jnp.zeros_like(pair)
    return jnp.concatenate([jnp.where(low, pair, zero), jnp.where(low, zero, pair)], axis=0)


def attention_kernel(
    tokens_ref,
    gain_one_ref,
    shift_one_ref,
    query_w_ref,
    key_w_ref,
    value_w_ref,
    out_w_ref,
    gain_two_ref,
    shift_two_ref,
    spread_ref,
    resid_ref,
    normed_ref,
    query_ref,
    key_ref,
    value_ref,
    weight_ref,
    mixed_ref,
    sent_ref,
):
    count, width = tokens_ref.shape
    inputs = tokens_ref[...].astype(F32)
    hat, _ = norm_rows(inputs)
    normed_ref[...] = (hat * gain_one_ref[...] + shift_one_ref[...]).astype(BF16)
    normed = normed_ref[...]
    query_ref[...] = (dot(normed, query_w_ref[...]).astype(BF16).astype(F32) * (1.0 / math.sqrt(width // HEADS))).astype(BF16)
    key_ref[...] = dot(normed, key_w_ref[...]).astype(BF16)
    value_ref[...] = dot(normed, value_w_ref[...]).astype(BF16)
    pairs = HEADS // 2
    wide = width // pairs
    block = 2 * PATCHES
    low = head_masks(wide)
    row_image = (lax.broadcasted_iota(jnp.int32, (2 * block, block), 0) % block) // PATCHES
    column_image = lax.broadcasted_iota(jnp.int32, (2 * block, block), 1) // PATCHES
    bias = jnp.where(row_image == column_image, 0.0, -1e30)
    for item in range(count // block):
        rows = slice(item * block, (item + 1) * block)
        for pair in range(pairs):
            lanes = slice(pair * wide, (pair + 1) * wide)
            stacked = stack_heads(query_ref[rows, lanes], low)
            scores = dot_nt(stacked, key_ref[rows, lanes]) + bias
            powers = jnp.exp(scores - jnp.max(scores, axis=-1, keepdims=True))
            weights = (powers / jnp.sum(powers, axis=-1, keepdims=True)).astype(BF16)
            weight_ref[item, pair] = weights
            mixed = dot(weights, value_ref[rows, lanes])
            mixed_ref[rows, lanes] = jnp.where(low, mixed[:block], mixed[block:]).astype(BF16)
    resid = inputs + dot(mixed_ref[...], out_w_ref[...])
    resid_ref[...] = resid
    hat, _ = norm_rows(resid)
    second = (hat * gain_two_ref[...] + shift_two_ref[...]).astype(BF16)
    sent_ref[...] = dot(spread_ref[...], second).astype(BF16)


def expert_kernel(
    experts,
    me_ref,
    rows_ref,
    grad_ref,
    up_ref,
    up_bias_ref,
    down_ref,
    down_bias_ref,
    router_ref,
    hidden_ref,
    inner_grad_ref,
    rows_grad_ref,
    gated_ref,
    gate_ref,
    router_grad_ref,
    inner_s,
    back_s,
    total_s,
    pair_s,
    gates_s,
):
    step = pl.program_id(0)
    total, width = rows_ref.shape
    tile = up_ref.shape[1]

    @pl.when(step == 0)
    def _():
        lane = lax.broadcasted_iota(jnp.int32, (total, LANES), 1)
        logits = dot_nt(rows_ref[...], router_ref[...])
        logits = jnp.where(lane < experts, logits, -1e30)
        powers = jnp.exp(logits - jnp.max(logits, axis=-1, keepdims=True))
        gates = powers / jnp.sum(powers, axis=-1, keepdims=True)
        gates_s[...] = gates
        gate = jnp.sum(jnp.where(lane == me_ref[0], gates, 0.0), axis=-1, keepdims=True)
        gate_ref[...] = jnp.broadcast_to(gate, (total, LANES))
        gated_ref[...] = (gate * grad_ref[...].astype(F32)).astype(BF16)
        total_s[...] = jnp.zeros_like(total_s)
        pair_s[...] = jnp.zeros_like(pair_s)

    inner_s[...] = dot(rows_ref[...], up_ref[...])
    back_s[...] = dot_nt(grad_ref[...], down_ref[...])
    chunk = 16
    root = math.sqrt(2.0 / math.pi)

    def some_rows(index, carry):
        at = pl.ds(pl.multiple_of(index * chunk, chunk), chunk)
        inner = inner_s[at, :] + up_bias_ref[...]
        back = back_s[at, :]
        square = inner * inner
        half = 0.5 + 0.5 * jnp.tanh(inner * (root + (root * 0.044715) * square))
        hidden = inner * half
        slope = half + (hidden - hidden * half) * (2.0 * root + (6.0 * root * 0.044715) * square)
        gate = gate_ref[at, :]
        gate = jnp.concatenate([gate] * (tile // LANES), axis=1)
        hidden_ref[at, :] = hidden.astype(BF16)
        inner_grad_ref[at, :] = (back * gate * slope).astype(BF16)
        product = hidden * back
        part = product[:, :LANES]
        for other in range(1, tile // LANES):
            part = part + product[:, other * LANES : (other + 1) * LANES]
        pair_s[at, :] = pair_s[at, :] + part
        return carry

    lax.fori_loop(0, total // chunk, some_rows, 0, unroll=2)
    total_s[...] += dot_nt(inner_grad_ref[...], up_ref[...])

    @pl.when(step == pl.num_programs(0) - 1)
    def _():
        lane = lax.broadcasted_iota(jnp.int32, (total, LANES), 1)
        pair_grad = jnp.sum(pair_s[...], axis=-1, keepdims=True)
        pair_grad = pair_grad + jnp.sum(grad_ref[...].astype(F32) * down_bias_ref[...], axis=-1, keepdims=True)
        own = jnp.where(lane == me_ref[0], 1.0, 0.0)
        logit_grad = (gates_s[...] * (own - gate_ref[...]) * pair_grad).astype(BF16)
        rows_grad_ref[...] = (total_s[...] + dot(logit_grad, router_ref[...])).astype(BF16)
        router_grad_ref[...] = dot_tn(logit_grad, rows_ref[...])


def weight_kernel(core_ref, rows_ref, gated_ref, hidden_ref, inner_grad_ref, keep_ref, send_ref):
    step = pl.program_id(0)
    width = rows_ref.shape[1]
    half = width // 2
    first = core_ref[0] == 0
    up = dot_tn(rows_ref[...], inner_grad_ref[...]).astype(BF16)
    keep_ref[0, :half, :] = jnp.where(first, up[:half], up[half:])
    send_ref[0, :half, :] = jnp.where(first, up[half:], up[:half])
    down = dot_tn(hidden_ref[...], gated_ref[...]).astype(BF16)
    keep_ref[0, half : 2 * half, :] = jnp.where(first, down[:half], down[half:])
    send_ref[0, half : 2 * half, :] = jnp.where(first, down[half:], down[:half])
    up_bias = jnp.sum(inner_grad_ref[...].astype(F32), axis=0, keepdims=True)
    down_bias = jnp.sum(gated_ref[...].astype(F32), axis=0, keepdims=True)
    small = jnp.concatenate([up_bias, down_bias, jnp.zeros((14, width), F32)], axis=0).astype(BF16)
    keep_ref[0, 2 * half :, :] = small
    send_ref[0, 2 * half :, :] = small


def produce_kernel(hidden_ref, down_ref, down_bias_ref, gate_ref, out_ref, total_s):
    step = pl.program_id(0)

    @pl.when(step == 0)
    def _():
        total_s[...] = jnp.zeros_like(total_s)

    total_s[...] += dot(hidden_ref[...], down_ref[...])

    @pl.when(step == pl.num_programs(0) - 1)
    def _():
        gate = gate_ref[...]
        gate = jnp.concatenate([gate] * (out_ref.shape[1] // LANES), axis=1)
        out_ref[...] = ((total_s[...] + down_bias_ref[...]) * gate).astype(BF16)


def add_kernel(one_ref, two_ref, out_ref):
    out_ref[...] = (one_ref[...].astype(F32) + two_ref[...].astype(F32)).astype(BF16)


def finish_experts_kernel(core_ref, own_ref, other_ref, up_ref, up_bias_ref, down_ref, down_bias_ref):
    half = up_ref.shape[0] // 2
    first = core_ref[0] == 0
    own = own_ref[0].astype(F32)
    other = other_ref[0].astype(F32)
    up_ref[:half, :] = jnp.where(first, own[:half], other[:half])
    up_ref[half:, :] = jnp.where(first, other[:half], own[:half])
    down_ref[:half, :] = jnp.where(first, own[half : 2 * half], other[half : 2 * half])
    down_ref[half:, :] = jnp.where(first, other[half : 2 * half], own[half : 2 * half])
    up_bias_ref[...] = own[2 * half : 2 * half + 1]
    down_bias_ref[...] = own[2 * half + 1 : 2 * half + 2]


def one_hot_rows(target_ref, slots_all):
    count = target_ref.shape[0]
    lane = lax.broadcasted_iota(jnp.int32, (64, slots_all), 1).astype(F32)
    pieces = []
    for start in range(0, count, 64):
        one = target_ref[start : start + 64, 0:1]
        two = target_ref[start : start + 64, 1:2]
        pieces.append(jnp.where((lane == one) | (lane == two), 1.0, 0.0).astype(BF16))
    return jnp.concatenate(pieces, axis=0)


def combine_kernel(target_ref, produced_ref, resid_ref, out_ref):
    picked = one_hot_rows(target_ref, produced_ref.shape[0])
    out_ref[...] = (resid_ref[...] + dot(picked, produced_ref[...])).astype(BF16)


def backward_kernel(
    experts,
    core_ref,
    target_ref,
    back_ref,
    resid_ref,
    grad_ref,
    gain_two_ref,
    tokens_ref,
    gain_one_ref,
    query_w_ref,
    key_w_ref,
    value_w_ref,
    out_w_ref,
    normed_ref,
    query_ref,
    key_ref,
    value_ref,
    weight_ref,
    mixed_ref,
    count_ref,
    router_grad_ref,
    keep_ref,
    send_ref,
    tokens_grad_ref,
    queries_s,
    keys_s,
    values_s,
    mixed_grad_s,
    resid_grad_s,
):
    count, width = tokens_ref.shape
    picked = one_hot_rows(target_ref, back_ref.shape[0])
    second_grad = dot(picked, back_ref[...])
    hat, rate = norm_rows(resid_ref[...])
    gain_two_grad = jnp.sum(second_grad * hat, axis=0, keepdims=True)
    shift_two_grad = jnp.sum(second_grad, axis=0, keepdims=True)
    resid_grad_s[...] = grad_ref[...].astype(F32) + norm_back(hat, rate, gain_two_ref[...], second_grad)
    branch = resid_grad_s[...].astype(BF16)
    half = width // 2
    first = core_ref[0] == 0

    def put(at, value):
        value = value.astype(BF16)
        keep_ref[at * half : (at + 1) * half, :] = jnp.where(first, value[:half], value[half:])
        send_ref[at * half : (at + 1) * half, :] = jnp.where(first, value[half:], value[:half])

    put(3, dot_tn(mixed_ref[...], branch))
    mixed_grad_s[...] = dot_nt(branch, out_w_ref[...]).astype(BF16)
    pairs = HEADS // 2
    wide = width // pairs
    block = 2 * PATCHES
    scale = 1.0 / math.sqrt(width // HEADS)
    low = head_masks(wide)
    for item in range(count // block):
        rows = slice(item * block, (item + 1) * block)
        for pair in range(pairs):
            lanes = slice(pair * wide, (pair + 1) * wide)
            mixed_stack = stack_heads(mixed_grad_s[rows, lanes], low)
            query_stack = stack_heads(query_ref[rows, lanes], low)
            weights = weight_ref[item, pair]
            weight_grad = dot_nt(mixed_stack, value_ref[rows, lanes])
            product = weights.astype(F32) * weight_grad
            score_grad = product - weights.astype(F32) * jnp.sum(product, axis=-1, keepdims=True)
            score_grad = score_grad.astype(BF16)
            values_s[rows, lanes] = dot_tn(weights, mixed_stack).astype(BF16)
            keys_s[rows, lanes] = dot_tn(score_grad, query_stack).astype(BF16)
            made = dot(score_grad, key_ref[rows, lanes]) * scale
            queries_s[rows, lanes] = jnp.where(low, made[:block], made[block:]).astype(BF16)
    normed = normed_ref[...]
    put(0, dot_tn(normed, queries_s[...]))
    put(1, dot_tn(normed, keys_s[...]))
    put(2, dot_tn(normed, values_s[...]))
    normed_grad = (
        dot_nt(queries_s[...], query_w_ref[...])
        + dot_nt(keys_s[...], key_w_ref[...])
        + dot_nt(values_s[...], value_w_ref[...])
    )
    hat, rate = norm_rows(tokens_ref[...].astype(F32))
    gain_one_grad = jnp.sum(normed_grad * hat, axis=0, keepdims=True)
    shift_one_grad = jnp.sum(normed_grad, axis=0, keepdims=True)
    tokens_grad_ref[...] = (resid_grad_s[...] + norm_back(hat, rate, gain_one_ref[...], normed_grad)).astype(BF16)
    digits = []
    for kind in range(2):
        value = count_ref[kind : kind + 1, :]
        high = jnp.floor(value * (1.0 / 128.0))
        digits.append(jnp.concatenate([value - 128.0 * high, high] + [jnp.zeros_like(value)] * (width // LANES - 2), axis=1))
    extra = keep_ref.shape[0] - 4 * half
    small = [gain_one_grad, shift_one_grad, gain_two_grad, shift_two_grad] + digits + [router_grad_ref[:experts, :]]
    small = jnp.concatenate(small + [jnp.zeros((extra - 6 - experts, width), F32)], axis=0).astype(BF16)
    keep_ref[4 * half :, :] = small
    send_ref[4 * half :, :] = small


def carry_digits(total):
    row = lax.broadcasted_iota(jnp.int32, (total.shape[0], LANES), 0)
    one, two, three = (total[:, at * LANES : (at + 1) * LANES] for at in range(3))
    over = jnp.floor(one * (1.0 / 128.0))
    two_full = two + over
    over_two = jnp.floor(two_full * (1.0 / 128.0))
    parts = [one - 128.0 * over, two_full - 128.0 * over_two, three + over_two]
    is_count = (row == 4) | (row == 5)
    parts = [jnp.where(is_count, part, total[:, at * LANES : (at + 1) * LANES]) for at, part in enumerate(parts)]
    return jnp.concatenate(parts + [total[:, 3 * LANES :]], axis=1)


def sum_in_tree(values):
    while len(values) > 1:
        values = [values[at] + values[at + 1] for at in range(0, len(values), 2)]
    return values[0]


def share_kernel(given, pieces, *refs):
    index_ref, arrived, made = refs[0], refs[1 : 1 + given], refs[1 + given :]
    small_rows = (pieces * made[0].shape[0] - arrived[0].shape[0]) // (pieces - 1)
    size = made[0].shape[0] - small_rows
    top = pieces * size
    small = carry_digits(sum_in_tree([ref[top:, :].astype(F32) for ref in arrived])).astype(BF16)
    for away in range(pieces):
        at = pl.ds(pl.multiple_of((index_ref[0] ^ away) * size, size), size)
        made[away][:size, :] = sum_in_tree([ref[at, :].astype(F32) for ref in arrived]).astype(BF16)
        made[away][size:, :] = small


def last_kernel(given, *refs):
    arrived, chunk_ref, small_ref = refs[:given], refs[given], refs[given + 1]
    size = chunk_ref.shape[0]
    chunk_ref[...] = sum_in_tree([ref[:size, :].astype(F32) for ref in arrived]).astype(BF16)
    small_ref[...] = carry_digits(sum_in_tree([ref[size:, :].astype(F32) for ref in arrived])).astype(BF16)


def finish_shared_kernel(experts, index_ref, own_ref, other_ref, small_ref, *outs):
    query_ref, key_ref, value_ref, out_ref, vector_refs, router_ref, count_ref = outs[:4] + (outs[4:8],) + outs[8:]
    core, place, inner_place = index_ref[0], index_ref[1], index_ref[2]
    width = query_ref.shape[1]
    half = width // 2
    size = half // 4
    for source, side in ((own_ref, core), (other_ref, 1 - core)):
        for at, out in enumerate((query_ref, key_ref, value_ref, out_ref)):
            for part in range(4):
                start = pl.multiple_of((place ^ at) * half + (inner_place ^ part) * size, size)
                row = pl.multiple_of(side * half + part * size, size)
                out[pl.ds(row, size), :] = source[pl.ds(start, size), :].astype(F32)
    small = small_ref[...].astype(F32)
    for at, ref in enumerate(vector_refs):
        ref[...] = small[at : at + 1, :]
    router_ref[...] = small[6 : 6 + experts, :]
    value = small[4:6, :LANES] + 128.0 * small[4:6, LANES : 2 * LANES] + 16384.0 * small[4:6, 2 * LANES : 3 * LANES]
    count_ref[...] = value[:, :experts].astype(jnp.int32)


def solution(mesh):
    narrow, wide = mesh.shape["narrow"], mesh.shape["wide"]

    def hop(value, narrow_bits, wide_bits):
        if wide_bits == 0:
            return lax.ppermute(value, "narrow", [(i, i ^ narrow_bits) for i in range(narrow)])
        if narrow_bits == 0:
            return lax.ppermute(value, "wide", [(i, i ^ wide_bits) for i in range(wide)])
        pairs = [
            (i * wide + j, (i ^ narrow_bits) * wide + (j ^ wide_bits)) for i in range(narrow) for j in range(wide)
        ]
        return lax.ppermute(value, ("narrow", "wide"), pairs)

    def body(
        tokens,
        gain_one,
        shift_one,
        query_w,
        key_w,
        value_w,
        out_w,
        gain_two,
        shift_two,
        router_w,
        up_w,
        up_bias,
        down_w,
        down_bias,
        picks,
        ranks,
        out_grad,
    ):
        count, width = tokens.shape
        experts = router_w.shape[1]
        capacity = ((21 * 2 * count + 20 * experts - 1) // (20 * experts) + 7) // 8 * 8
        slots_all = experts * capacity
        hidden_width = up_w.shape[2]
        half = width // 2
        pairs = HEADS // 2
        blocks = count // (2 * PATCHES)
        extra = (6 + experts + 15) // 16 * 16
        tile = width
        steps = hidden_width // tile
        narrow_at, wide_at = lax.axis_index("narrow"), lax.axis_index("wide")
        core = (narrow_at & 1)[None].astype(jnp.int32)
        place = (((narrow_at >> 1) & 1) * 2 + (wide_at & 1))[None].astype(jnp.int32)
        inner_place = ((wide_at >> 1) & 3)[None].astype(jnp.int32)
        gain_one, shift_one, gain_two, shift_two = (v[None, :] for v in (gain_one, shift_one, gain_two, shift_two))
        router_t = jnp.pad(router_w.T, ((0, LANES - experts), (0, 0)))
        up_w, down_w = up_w[0], down_w[0]

        def exchange(value):
            return lax.all_to_all(value, "wide", split_axis=0, concat_axis=0, tiled=True)

        spread, target, counts, grad_sent = pl.pallas_call(
            functools.partial(route_kernel, capacity, experts),
            out_shape=(
                shape((slots_all, count), BF16),
                shape((count, 8), F32),
                shape((8, LANES), F32),
                shape((slots_all, width), BF16),
            ),
            compiler_params=params(24),
            cost_estimate=cost(3),
            name="route",
        )(picks.T, ranks.T, out_grad)
        grad_rows = exchange(grad_sent)

        resid, normed, queries, keys, values, weights, mixed, sent = pl.pallas_call(
            attention_kernel,
            out_shape=(
                shape((count, width), F32),
                shape((count, width), BF16),
                shape((count, width), BF16),
                shape((count, width), BF16),
                shape((count, width), BF16),
                shape((blocks, pairs, 4 * PATCHES, 2 * PATCHES), BF16),
                shape((count, width), BF16),
                shape((slots_all, width), BF16),
            ),
            compiler_params=params(32),
            cost_estimate=cost(10),
            name="attention",
        )(tokens, gain_one, shift_one, query_w, key_w, value_w, out_w, gain_two, shift_two, spread)
        rows = exchange(sent)

        whole = pl.BlockSpec((slots_all, width), lambda f: (0, 0))
        lanes_whole = pl.BlockSpec((slots_all, LANES), lambda f: (0, 0))
        columns = pl.BlockSpec((slots_all, tile), lambda f: (0, f))
        up_spec = pl.BlockSpec((width, tile), lambda f: (0, f))
        down_spec = pl.BlockSpec((tile, width), lambda f: (f, 0))
        up_bias_spec = pl.BlockSpec((1, tile), lambda f: (0, f))
        down_bias_spec = pl.BlockSpec((1, width), lambda f: (0, 0))
        router_spec = pl.BlockSpec((LANES, width), lambda f: (0, 0))
        hidden, inner_grad, rows_grad, gated, gate, router_part = pl.pallas_call(
            functools.partial(expert_kernel, experts),
            grid=(steps,),
            in_specs=[SMEM(), whole, whole, up_spec, up_bias_spec, down_spec, down_bias_spec, router_spec],
            out_specs=(columns, columns, whole, whole, lanes_whole, router_spec),
            out_shape=(
                shape((slots_all, hidden_width), BF16),
                shape((slots_all, hidden_width), BF16),
                shape((slots_all, width), BF16),
                shape((slots_all, width), BF16),
                shape((slots_all, LANES), F32),
                shape((LANES, width), F32),
            ),
            scratch_shapes=[
                pltpu.VMEM((slots_all, tile), F32),
                pltpu.VMEM((slots_all, tile), F32),
                pltpu.VMEM((slots_all, width), F32),
                pltpu.VMEM((slots_all, LANES), F32),
                pltpu.VMEM((slots_all, LANES), F32),
            ],
            compiler_params=params(40),
            cost_estimate=cost(10),
            name="experts",
        )(wide_at[None].astype(jnp.int32), rows, grad_rows, up_w, up_bias, down_w, down_bias, router_t)
        back = exchange(rows_grad)

        payload = 2 * half + 16
        payload_spec = pl.BlockSpec((1, payload, width), lambda f: (f, 0, 0))
        keep, send = pl.pallas_call(
            weight_kernel,
            grid=(steps,),
            in_specs=[SMEM(), whole, whole, columns, columns],
            out_specs=(payload_spec, payload_spec),
            out_shape=(shape((steps, payload, width), BF16),) * 2,
            compiler_params=params(40),
            cost_estimate=cost(6),
            name="expert_weights",
        )(core, rows, gated, hidden, inner_grad)
        produced = pl.pallas_call(
            produce_kernel,
            grid=(steps,),
            in_specs=[columns, down_spec, down_bias_spec, lanes_whole],
            out_specs=whole,
            out_shape=shape((slots_all, width), BF16),
            scratch_shapes=[pltpu.VMEM((slots_all, width), F32)],
            compiler_params=params(32),
            cost_estimate=cost(4),
            name="produce",
        )(hidden, down_w, down_bias, gate)

        def add(one, two):
            return pl.pallas_call(
                add_kernel,
                grid=(steps,),
                in_specs=[payload_spec, payload_spec],
                out_specs=payload_spec,
                out_shape=shape((steps, payload, width), BF16),
                compiler_params=params(16),
                cost_estimate=cost(2),
                name="add_halves",
            )(one, two)

        expert_sum = add(keep, hop(send, 1, 0))
        bit = 2
        while bit < narrow:
            expert_sum = add(expert_sum, hop(expert_sum, bit, 0))
            bit *= 2
        up_grad, up_bias_grad, down_grad, down_bias_grad = pl.pallas_call(
            finish_experts_kernel,
            grid=(steps,),
            in_specs=[SMEM(), payload_spec, payload_spec],
            out_specs=(up_spec, up_bias_spec, down_spec, down_bias_spec),
            out_shape=(
                shape((width, hidden_width), F32),
                shape((1, hidden_width), F32),
                shape((hidden_width, width), F32),
                shape((1, width), F32),
            ),
            compiler_params=params(24),
            cost_estimate=cost(4),
            name="finish_experts",
        )(core, expert_sum, hop(expert_sum, 1, 0))

        produced_back = exchange(produced)
        block_out = pl.pallas_call(
            combine_kernel,
            out_shape=shape((count, width), BF16),
            compiler_params=params(16),
            cost_estimate=cost(2),
            name="combine",
        )(target, produced_back, resid)

        tall = 4 * half + extra
        keep, send, tokens_grad = pl.pallas_call(
            functools.partial(backward_kernel, experts),
            in_specs=[SMEM()] + [VMEM()] * 19,
            out_shape=(shape((tall, width), BF16), shape((tall, width), BF16), shape((count, width), BF16)),
            scratch_shapes=[pltpu.VMEM((count, width), BF16)] * 4 + [pltpu.VMEM((count, width), F32)],
            compiler_params=params(32),
            cost_estimate=cost(12),
            name="backward",
        )(
            core,
            target,
            back,
            resid,
            out_grad,
            gain_two,
            tokens,
            gain_one,
            query_w,
            key_w,
            value_w,
            out_w,
            normed,
            queries,
            keys,
            values,
            weights,
            mixed,
            counts,
            router_part,
        )

        def share(index, arrived):
            size = (arrived[0].shape[0] - extra) // 4
            return pl.pallas_call(
                functools.partial(share_kernel, len(arrived), 4),
                in_specs=[SMEM()] + [VMEM()] * len(arrived),
                out_shape=(shape((size + extra, width), BF16),) * 4,
                compiler_params=params(16),
                cost_estimate=cost(1),
                name="share",
            )(index, *arrived)

        places = ((0, 0), (0, 1), (2, 0), (2, 1))
        inner_places = ((0, 0), (0, 2), (0, 4), (0, 6))
        parts = share(place, [keep, hop(send, 1, 0)])
        parts = [parts[0]] + [hop(part, *bits) for part, bits in zip(parts[1:], places[1:])]
        parts = share(inner_place, parts)
        parts = [parts[0]] + [hop(part, *bits) for part, bits in zip(parts[1:], inner_places[1:])]

        def last(arrived):
            size = half // 4
            return pl.pallas_call(
                functools.partial(last_kernel, len(arrived)),
                out_shape=(shape((size, width), BF16), shape((extra, width), BF16)),
                compiler_params=params(16),
                cost_estimate=cost(1),
                name="last",
            )(*arrived)

        chunk, small = last(parts)
        others = [(bit, 0) for bit in (4, 8, 16, 32, 64) if bit < narrow]
        others += [(0, bit) for bit in (8, 16, 32, 64) if bit < wide]
        for bits in others:
            joined = jnp.concatenate([chunk, small], axis=0)
            chunk, small = last([joined, hop(joined, *bits)])
        chunk = jnp.concatenate([chunk] + [hop(chunk, *bits) for bits in inner_places[1:]], axis=0)
        chunk = jnp.concatenate([chunk] + [hop(chunk, *bits) for bits in places[1:]], axis=0)
        outs = pl.pallas_call(
            functools.partial(finish_shared_kernel, experts),
            in_specs=[SMEM()] + [VMEM()] * 3,
            out_shape=(shape((width, width), F32),) * 4
            + (shape((1, width), F32),) * 4
            + (shape((experts, width), F32), shape((2, experts), jnp.int32)),
            compiler_params=params(24),
            cost_estimate=cost(3),
            name="finish_shared",
        )(jnp.concatenate([core, place, inner_place]), chunk, hop(chunk, 1, 0), small)
        query_grad, key_grad, value_grad, out_w_grad, g_one, s_one, g_two, s_two, router_grad, tallies = outs
        return (
            block_out,
            tokens_grad,
            g_one[0],
            s_one[0],
            query_grad,
            key_grad,
            value_grad,
            out_w_grad,
            g_two[0],
            s_two[0],
            router_grad.T,
            up_grad[None],
            up_bias_grad,
            down_grad[None],
            down_bias_grad,
            tallies.T,
        )

    tokens_spec = P(("narrow", "wide"), None)
    in_specs = (
        (tokens_spec,)
        + (P(),) * 9
        + (P("wide", None, None), P("wide", None), P("wide", None, None), P("wide", None))
        + (tokens_spec,) * 3
    )
    out_specs = (
        (tokens_spec,) * 2
        + (P(),) * 9
        + (P("wide", None, None), P("wide", None), P("wide", None, None), P("wide", None))
        + (P(),)
    )
    return jax.shard_map(body, mesh=mesh, in_specs=in_specs, out_specs=out_specs, check_vma=False)
```

profile of v0, /device:TPU:0, one launch (start us, length us, event | category | flops | bytes accessed | tf_op | source)
XLA Modules:
  0.0 262.0 jit_solution(17795780976494734319)
XLA Ops:
  3.1 2.3 route.1
  6.9 7.3 %all-to-all-start.1 = ((bf16[8,104,512]{2,1,0:T(8,128)(2,1)}), bf16[8,104,512]{2,1,0:T(8,128)(2,1)S(1)}, u32[]{:S(2)}, u32[]{:S(2)}) async-start(bf16[8,104,512]{2,1,0:T(8,128)(2,1)} %bitcast.9), calls=%async_computation.1 | async-start | bytes 1703936 | tf_op jit(solution)/shard_map/all_to_all | solution.py:511
  15.4 4.0 %attention.1 = (f32[384,512]{1,0:T(8,128)S(1)}, bf16[384,512]{1,0:T(8,128)(2,1)S(1)}, bf16[384,512]{1,0:T(8,128)(2,1)S(1)}, bf16[384,512]{1,0:T(8,128)(2,1)S(1)}...) custom-call(bf16[384,512]{1,0:T(8,128)(2,1)S(1)} %copy-done.12, ...), custom_call_target="tpu_custom_call" | custom-call | flops 10000000000 | bytes 10000000 | tf_op jit(solution)/shard_map/attention/pallas_call | solution.py:527
  24.9 10.9 %all-to-all-done.1 = bf16[8,104,512]{2,1,0:T(8,128)(2,1)S(1)} async-done(((bf16[8,104,512]{2,1,0:T(8,128)(2,1)}), bf16[8,104,512]{2,1,0:T(8,128)(2,1)S(1)}, u32[]{:S(2)}, u32[]{:S(2)}) %all-to-all-start.1) | async-done | bytes 852000 | tf_op jit(solution)/shard_map/all_to_all | solution.py:511
  35.8 3.6 %all-to-all-start = ((bf16[8,104,512]{2,1,0:T(8,128)(2,1)}), bf16[8,104,512]{2,1,0:T(8,128)(2,1)S(1)}, u32[]{:S(2)}, u32[]{:S(2)}) async-start(bf16[8,104,512]{2,1,0:T(8,128)(2,1)} %bitcast.7), calls=%async_computation | async-start | bytes 1703936 | tf_op jit(solution)/shard_map/all_to_all | solution.py:511
  39.4 21.7 %all-to-all-done = bf16[8,104,512]{2,1,0:T(8,128)(2,1)S(1)} async-done(((bf16[8,104,512]{2,1,0:T(8,128)(2,1)}), bf16[8,104,512]{2,1,0:T(8,128)(2,1)S(1)}, u32[]{:S(2)}, u32[]{:S(2)}) %all-to-all-start) | async-done | bytes 852000 | tf_op jit(solution)/shard_map/all_to_all | solution.py:511
  64.3 15.1 %experts.1 = (bf16[832,2048]{1,0:T(8,128)(2,1)S(1)}, bf16[832,2048]{1,0:T(8,128)(2,1)}, bf16[832,512]{1,0:T(8,128)(2,1)}, bf16[832,512]{1,0:T(8,128)(2,1)S(1)}, ...) custom-call(s32[1]{0:T(128)} %bitcast.2.me_ref, bf16[832,512]{1,0:T(8,128)(2,1)S(1)} %bitcast.31, ...), custom_call_target="tpu_custom_call" | custom-call | flops 10000000000 | bytes 10000000 | tf_op jit(solution)/shard_map/experts/pallas_call | solution.py:553
  82.6 3.7 %all-to-all-start.3 = ((bf16[8,104,512]{2,1,0:T(8,128)(2,1)}), bf16[8,104,512]{2,1,0:T(8,128)(2,1)S(1)}, u32[]{:S(2)}, u32[]{:S(2)}) async-start(bf16[8,104,512]{2,1,0:T(8,128)(2,1)} %bitcast.17), calls=%async_computation.3 | async-start | bytes 1703936 | tf_op jit(solution)/shard_map/all_to_all | solution.py:511
  90.3 7.1 %expert_weights.1 = (bf16[4,528,512]{2,1,0:T(8,128)(2,1)S(1)}, bf16[4,528,512]{2,1,0:T(8,128)(2,1)}) custom-call(s32[1]{0:T(128)} %bitcast.16.core_ref, bf16[832,512]{1,0:T(8,128)(2,1)S(1)} %bitcast.32, bf16[832,512]{1,0:T(8,128)(2,1)S(1)} %get-tuple-element.101.gated_ref, bf16[832,2048]{1,0:T(8,128)(2,1)S(1)} %copy-done.29, bf16[832,2048]{1,0:T(8,128)(2,1)S(1)} %copy-done.34), custom_call_target="tpu_custom_call" | custom-call | flops 6000000000 | bytes 6000000 | tf_op jit(solution)/shard_map/expert_weights/pallas_call | solution.py:581
  98.7 9.3 %all-to-all-done.3 = bf16[8,104,512]{2,1,0:T(8,128)(2,1)S(1)} async-done(((bf16[8,104,512]{2,1,0:T(8,128)(2,1)}), bf16[8,104,512]{2,1,0:T(8,128)(2,1)S(1)}, u32[]{:S(2)}, u32[]{:S(2)}) %all-to-all-start.3) | async-done | bytes 852000 | tf_op jit(solution)/shard_map/all_to_all | solution.py:511
  122.3 9.2 %backward.1 = (bf16[1040,512]{1,0:T(8,128)(2,1)S(1)}, bf16[1040,512]{1,0:T(8,128)(2,1)}, bf16[384,512]{1,0:T(8,128)(2,1)}) custom-call(s32[1]{0:T(128)} %bitcast.16.core_ref, f32[384,8]{1,0:T(8,128)S(1)} %copy-done.36, bf16[832,512]{1,0:T(8,128)(2,1)S(1)} %bitcast.33, f32[384,512]{1,0:T(8,128)S(1)} %copy-done.32, bf16[384,512]{1,0:T(8,128)(2,1)S(1)} %copy-done.11, ...), custom_call_target="tpu_custom_call" | custom-call | flops 12000000000 | bytes 12000000 | tf_op jit(solution)/shard_map/backward/pallas_call | solution.py:646
  142.7 5.3 %collective-permute-done.1.refs_2_ = bf16[272,512]{1,0:T(8,128)(2,1)S(1)} collective-permute-done((bf16[272,512]{1,0:T(8,128)(2,1)}, bf16[272,512]{1,0:T(8,128)(2,1)S(1)}, u32[]{:S(2)}, u32[]{:S(2)}) %collective-permute-start.1) | collective-permute-done | bytes 278560 | tf_op jit(solution)/shard_map/ppermute | solution.py:466
  148.0 41.7 %collective-permute-done.2.refs_3_ = bf16[272,512]{1,0:T(8,128)(2,1)S(1)} collective-permute-done((bf16[272,512]{1,0:T(8,128)(2,1)S(1)}, bf16[272,512]{1,0:T(8,128)(2,1)S(1)}, u32[]{:S(2)}, u32[]{:S(2)}) %collective-permute-start.2) | collective-permute-done | bytes 278560 | tf_op jit(solution)/shard_map/ppermute | solution.py:464
  189.7 6.1 %collective-permute-done.3.refs_4_ = bf16[272,512]{1,0:T(8,128)(2,1)S(1)} collective-permute-done((bf16[272,512]{1,0:T(8,128)(2,1)S(1)}, bf16[272,512]{1,0:T(8,128)(2,1)S(1)}, u32[]{:S(2)}, u32[]{:S(2)}) %collective-permute-start.3) | collective-permute-done | bytes 278560 | tf_op jit(solution)/shard_map/ppermute | solution.py:470
  203.3 3.9 %produce.1 = bf16[832,512]{1,0:T(8,128)(2,1)} custom-call(bf16[832,2048]{1,0:T(8,128)(2,1)S(1)} %copy-done.30, bf16[2048,512]{1,0:T(8,128)(2,1)S(1)} %bitcast.36, f32[1,512]{1,0:T(1,128)S(1)} %copy-done.21, f32[832,128]{1,0:T(8,128)S(1)} %copy-done.39), custom_call_target="tpu_custom_call" | custom-call | flops 4000000000 | bytes 4000000 | tf_op jit(solution)/shard_map/produce/pallas_call | solution.py:591
  207.2 3.6 %all-to-all-start.2 = ((bf16[8,104,512]{2,1,0:T(8,128)(2,1)}), bf16[8,104,512]{2,1,0:T(8,128)(2,1)S(1)}, u32[]{:S(2)}, u32[]{:S(2)}) async-start(bf16[8,104,512]{2,1,0:T(8,128)(2,1)} %bitcast.14), calls=%async_computation.2 | async-start | bytes 1703936 | tf_op jit(solution)/shard_map/all_to_all | solution.py:511
  210.9 3.8 %collective-permute-start.9 = (bf16[64,512]{1,0:T(8,128)(2,1)S(1)}, bf16[64,512]{1,0:T(8,128)(2,1)S(1)}, u32[]{:S(2)}, u32[]{:S(2)}) collective-permute-start(bf16[64,512]{1,0:T(8,128)(2,1)S(1)} %get-tuple-element.90), channel_id=1, source_target_pairs={{0,6},{1,7},{2,4},{3,5},{4,2},{5,3},{6,0},{7,1},{8,14},{9,15},{10,... | collective-permute-start | bytes 196616 | tf_op jit(solution)/shard_map/ppermute | solution.py:466
  215.3 12.6 %collective-permute-done.7 = bf16[64,512]{1,0:T(8,128)(2,1)S(1)} collective-permute-done((bf16[64,512]{1,0:T(8,128)(2,1)S(1)}, bf16[64,512]{1,0:T(8,128)(2,1)S(1)}, u32[]{:S(2)}, u32[]{:S(2)}) %collective-permute-start.7) | collective-permute-done | bytes 65568 | tf_op jit(solution)/shard_map/ppermute | solution.py:466
  228.0 4.4 %add_halves.3.own_ref = bf16[4,528,512]{2,1,0:T(8,128)(2,1)} custom-call(bf16[4,528,512]{2,1,0:T(8,128)(2,1)} %add_halves.2.one_ref, bf16[4,528,512]{2,1,0:T(8,128)(2,1)} %collective-permute-done.15.two_ref), custom_call_target="tpu_custom_call" | custom-call | flops 2000000000 | bytes 2000000 | tf_op jit(solution)/shard_map/add_halves/pallas_call | solution.py:604
  232.4 4.7 %collective-permute-done.8 = bf16[64,512]{1,0:T(8,128)(2,1)S(1)} collective-permute-done((bf16[64,512]{1,0:T(8,128)(2,1)S(1)}, bf16[64,512]{1,0:T(8,128)(2,1)S(1)}, u32[]{:S(2)}, u32[]{:S(2)}) %collective-permute-start.8) | collective-permute-done | bytes 65568 | tf_op jit(solution)/shard_map/ppermute | solution.py:466
  240.8 4.9 %collective-permute-done.10 = bf16[256,512]{1,0:T(8,128)(2,1)S(1)} collective-permute-done((bf16[256,512]{1,0:T(8,128)(2,1)S(1)}, bf16[256,512]{1,0:T(8,128)(2,1)S(1)}, u32[]{:S(2)}, u32[]{:S(2)}) %collective-permute-start.10) | collective-permute-done | bytes 262176 | tf_op jit(solution)/shard_map/ppermute | solution.py:466
  247.8 2.6 %collective-permute-done.12 = bf16[256,512]{1,0:T(8,128)(2,1)S(1)} collective-permute-done((bf16[256,512]{1,0:T(8,128)(2,1)S(1)}, bf16[256,512]{1,0:T(8,128)(2,1)S(1)}, u32[]{:S(2)}, u32[]{:S(2)}) %collective-permute-start.12) | collective-permute-done | bytes 262176 | tf_op jit(solution)/shard_map/ppermute | solution.py:470
  253.2 2.8 %finish_shared.1 = (f32[512,512]{1,0:T(8,128)}, f32[512,512]{1,0:T(8,128)}, f32[512,512]{1,0:T(8,128)}, f32[512,512]{1,0:T(8,128)}, f32[1,512]{1,0:T(1,128)}, /*...) custom-call(s32[3]{0:T(128)S(1)} %pad_add_fusion.index_ref, ...), custom_call_target="tpu_custom_call" | custom-call | flops 3000000000 | bytes 3000000 | tf_op jit(solution)/shard_map/finish_shared/pallas_call | solution.py:713
  255.9 5.9 %finish_experts.1 = (f32[512,2048]{1,0:T(8,128)}, f32[1,2048]{1,0:T(1,128)}, f32[2048,512]{1,0:T(8,128)}, f32[1,512]{1,0:T(1,128)}) custom-call(s32[1]{0:T(128)} %bitcast.16.core_ref, bf16[4,528,512]{2,1,0:T(8,128)(2,1)} %add_halves.3.own_ref, bf16[4,528,512]{2,1,0:T(8,128)(2,1)} %collective-permute-done.16.other_ref), custom_call_target="tpu_custom_call" | custom-call | flops 4000000000 | bytes 4000000 | tf_op jit(solution)/shard_map/finish_experts/pallas_call | solution.py:620
  (155 shorter events, 64.3 us)
Async XLA Ops:
  6.9 28.9 %all-to-all-start.1 = ((bf16[8,104,512]{2,1,0:T(8,128)(2,1)}), bf16[8,104,512]{2,1,0:T(8,128)(2,1)S(1)}, u32[]{:S(2)}, u32[]{:S(2)}) async-start(bf16[8,104,512]{2,1,0:T(8,128)(2,1)} %bitcast.9), calls=%async_computation.1 | async-start | bytes 1703936 | tf_op jit(solution)/shard_map/all_to_all | solution.py:511
  15.4 45.7 %copy-start.14 = (f32[1,2048]{1,0:T(1,128)S(1)}, f32[1,2048]{1,0:T(1,128)}, u32[]{:S(2)}) copy-start(f32[1,2048]{1,0:T(1,128)} %up_bias_ref.1) | copy-start | bytes 24580
  15.4 45.7 %copy-start.21 = (f32[1,512]{1,0:T(1,128)S(1)}, f32[1,512]{1,0:T(1,128)}, u32[]{:S(2)}) copy-start(f32[1,512]{1,0:T(1,128)} %down_bias_ref.3) | copy-start | bytes 6148
  35.8 25.3 %all-to-all-start = ((bf16[8,104,512]{2,1,0:T(8,128)(2,1)}), bf16[8,104,512]{2,1,0:T(8,128)(2,1)S(1)}, u32[]{:S(2)}, u32[]{:S(2)}) async-start(bf16[8,104,512]{2,1,0:T(8,128)(2,1)} %bitcast.7), calls=%async_computation | async-start | bytes 1703936 | tf_op jit(solution)/shard_map/all_to_all | solution.py:511
  82.6 25.4 %all-to-all-start.3 = ((bf16[8,104,512]{2,1,0:T(8,128)(2,1)}), bf16[8,104,512]{2,1,0:T(8,128)(2,1)S(1)}, u32[]{:S(2)}, u32[]{:S(2)}) async-start(bf16[8,104,512]{2,1,0:T(8,128)(2,1)} %bitcast.17), calls=%async_computation.3 | async-start | bytes 1703936 | tf_op jit(solution)/shard_map/all_to_all | solution.py:511
  98.7 32.7 %collective-permute-start.14 = (bf16[4,528,512]{2,1,0:T(8,128)(2,1)}, bf16[4,528,512]{2,1,0:T(8,128)(2,1)S(1)}, u32[]{:S(2)}, u32[]{:S(2)}) collective-permute-start(bf16[4,528,512]{2,1,0:T(8,128)(2,1)} %get-tuple-element.104), channel_id=1, source_target_pairs={{0,8},{8,0},{16,24},{24,16},{1,9},{9,1},{17,25},{25,17},{2,10},{10... | collective-permute-start | bytes 6488072 | tf_op jit(solution)/shard_map/ppermute | solution.py:464
  131.4 3.8 %collective-permute-start = (bf16[1040,512]{1,0:T(8,128)(2,1)}, bf16[1040,512]{1,0:T(8,128)(2,1)}, u32[]{:S(2)}, u32[]{:S(2)}) collective-permute-start(bf16[1040,512]{1,0:T(8,128)(2,1)} %get-tuple-element.81), channel_id=1, source_target_pairs={{0,8},{8,0},{16,24},{24,16},{1,9},{9,1},{17,25},{25,17},{2,10},{10... | collective-permute-start | bytes 3194888 | tf_op jit(solution)/shard_map/ppermute | solution.py:464
  133.7 94.3 %collective-permute-start.15 = (bf16[4,528,512]{2,1,0:T(8,128)(2,1)}, bf16[4,528,512]{2,1,0:T(8,128)(2,1)}, u32[]{:S(2)}, u32[]{:S(2)}) collective-permute-start(bf16[4,528,512]{2,1,0:T(8,128)(2,1)} %add_halves.2.one_ref), channel_id=1, source_target_pairs={{0,16},{8,24},{16,0},{24,8},{1,17},{9,25},{17,1},{25,9},{2,18},{10... | collective-permute-start | bytes 6488072 | tf_op jit(solution)/shard_map/ppermute | solution.py:464
  139.2 62.2 %copy-start.2 = (bf16[1,2048,512]{2,1,0:T(8,128)(2,1)S(1)}, bf16[1,2048,512]{2,1,0:T(8,128)(2,1)}, u32[]{:S(2)}) copy-start(bf16[1,2048,512]{2,1,0:T(8,128)(2,1)} %param.29) | copy-start | bytes 6291460
  139.2 8.8 %collective-permute-start.1 = (bf16[272,512]{1,0:T(8,128)(2,1)}, bf16[272,512]{1,0:T(8,128)(2,1)S(1)}, u32[]{:S(2)}, u32[]{:S(2)}) collective-permute-start(bf16[272,512]{1,0:T(8,128)(2,1)} %get-tuple-element.83), channel_id=1, source_target_pairs={{0,1},{1,0},{2,3},{3,2},{4,5},{5,4},{6,7},{7,6},{8,9},{9,8},{10,11... | collective-permute-start | bytes 835592 | tf_op jit(solution)/shard_map/ppermute | solution.py:466
  140.6 49.1 %collective-permute-start.2 = (bf16[272,512]{1,0:T(8,128)(2,1)S(1)}, bf16[272,512]{1,0:T(8,128)(2,1)S(1)}, u32[]{:S(2)}, u32[]{:S(2)}) collective-permute-start(bf16[272,512]{1,0:T(8,128)(2,1)S(1)} %get-tuple-element.84), channel_id=1, source_target_pairs={{0,16},{8,24},{16,0},{24,8},{1,17},{9,25},{17,1},{25,9},{2,18},{10... | collective-permute-start | bytes 835592 | tf_op jit(solution)/shard_map/ppermute | solution.py:464
  141.3 54.5 %collective-permute-start.3 = (bf16[272,512]{1,0:T(8,128)(2,1)S(1)}, bf16[272,512]{1,0:T(8,128)(2,1)S(1)}, u32[]{:S(2)}, u32[]{:S(2)}) collective-permute-start(bf16[272,512]{1,0:T(8,128)(2,1)S(1)} %get-tuple-element.85), channel_id=1, source_target_pairs={{0,17},{1,16},{2,19},{3,18},{4,21},{5,20},{6,23},{7,22},{8,25},{9,... | collective-permute-start | bytes 835592 | tf_op jit(solution)/shard_map/ppermute | solution.py:470
  196.9 13.9 %collective-permute-start.4 = (bf16[80,512]{1,0:T(8,128)(2,1)S(1)}, bf16[80,512]{1,0:T(8,128)(2,1)S(1)}, u32[]{:S(2)}, u32[]{:S(2)}) collective-permute-start(bf16[80,512]{1,0:T(8,128)(2,1)S(1)} %get-tuple-element.87), channel_id=1, source_target_pairs={{0,2},{1,3},{2,0},{3,1},{4,6},{5,7},{6,4},{7,5},{8,10},{9,11},{10,... | collective-permute-start | bytes 245768 | tf_op jit(solution)/shard_map/ppermute | solution.py:466
  197.0 13.8 %collective-permute-start.5 = (bf16[80,512]{1,0:T(8,128)(2,1)S(1)}, bf16[80,512]{1,0:T(8,128)(2,1)S(1)}, u32[]{:S(2)}, u32[]{:S(2)}) collective-permute-start(bf16[80,512]{1,0:T(8,128)(2,1)S(1)} %get-tuple-element.88), channel_id=1, source_target_pairs={{0,4},{1,5},{2,6},{3,7},{4,0},{5,1},{6,2},{7,3},{8,12},{9,13},{10,... | collective-permute-start | bytes 245768 | tf_op jit(solution)/shard_map/ppermute | solution.py:466
  199.0 11.8 %collective-permute-start.6 = (bf16[80,512]{1,0:T(8,128)(2,1)S(1)}, bf16[80,512]{1,0:T(8,128)(2,1)S(1)}, u32[]{:S(2)}, u32[]{:S(2)}) collective-permute-start(bf16[80,512]{1,0:T(8,128)(2,1)S(1)} %get-tuple-element.89), channel_id=1, source_target_pairs={{0,6},{1,7},{2,4},{3,5},{4,2},{5,3},{6,0},{7,1},{8,14},{9,15},{10,... | collective-permute-start | bytes 245768 | tf_op jit(solution)/shard_map/ppermute | solution.py:466
  207.2 43.4 %all-to-all-start.2 = ((bf16[8,104,512]{2,1,0:T(8,128)(2,1)}), bf16[8,104,512]{2,1,0:T(8,128)(2,1)S(1)}, u32[]{:S(2)}, u32[]{:S(2)}) async-start(bf16[8,104,512]{2,1,0:T(8,128)(2,1)} %bitcast.14), calls=%async_computation.2 | async-start | bytes 1703936 | tf_op jit(solution)/shard_map/all_to_all | solution.py:511
  210.9 26.3 %collective-permute-start.9 = (bf16[64,512]{1,0:T(8,128)(2,1)S(1)}, bf16[64,512]{1,0:T(8,128)(2,1)S(1)}, u32[]{:S(2)}, u32[]{:S(2)}) collective-permute-start(bf16[64,512]{1,0:T(8,128)(2,1)S(1)} %get-tuple-element.90), channel_id=1, source_target_pairs={{0,6},{1,7},{2,4},{3,5},{4,2},{5,3},{6,0},{7,1},{8,14},{9,15},{10,... | collective-permute-start | bytes 196616 | tf_op jit(solution)/shard_map/ppermute | solution.py:466
  214.7 22.5 %collective-permute-start.8 = (bf16[64,512]{1,0:T(8,128)(2,1)S(1)}, bf16[64,512]{1,0:T(8,128)(2,1)S(1)}, u32[]{:S(2)}, u32[]{:S(2)}) collective-permute-start(bf16[64,512]{1,0:T(8,128)(2,1)S(1)} %get-tuple-element.90), channel_id=1, source_target_pairs={{0,4},{1,5},{2,6},{3,7},{4,0},{5,1},{6,2},{7,3},{8,12},{9,13},{10,... | collective-permute-start | bytes 196616 | tf_op jit(solution)/shard_map/ppermute | solution.py:466
  214.7 13.3 %collective-permute-start.7 = (bf16[64,512]{1,0:T(8,128)(2,1)S(1)}, bf16[64,512]{1,0:T(8,128)(2,1)S(1)}, u32[]{:S(2)}, u32[]{:S(2)}) collective-permute-start(bf16[64,512]{1,0:T(8,128)(2,1)S(1)} %get-tuple-element.90), channel_id=1, source_target_pairs={{0,2},{1,3},{2,0},{3,1},{4,6},{5,7},{6,4},{7,5},{8,10},{9,11},{10,... | collective-permute-start | bytes 196616 | tf_op jit(solution)/shard_map/ppermute | solution.py:466
  232.4 23.5 %collective-permute-start.16 = (bf16[4,528,512]{2,1,0:T(8,128)(2,1)}, bf16[4,528,512]{2,1,0:T(8,128)(2,1)}, u32[]{:S(2)}, u32[]{:S(2)}) collective-permute-start(bf16[4,528,512]{2,1,0:T(8,128)(2,1)} %add_halves.3.own_ref), channel_id=1, source_target_pairs={{0,8},{8,0},{16,24},{24,16},{1,9},{9,1},{17,25},{25,17},{2,10},{10... | collective-permute-start | bytes 6488072 | tf_op jit(solution)/shard_map/ppermute | solution.py:464
  237.2 8.5 %collective-permute-start.10 = (bf16[256,512]{1,0:T(8,128)(2,1)S(1)}, bf16[256,512]{1,0:T(8,128)(2,1)S(1)}, u32[]{:S(2)}, u32[]{:S(2)}) collective-permute-start(bf16[256,512]{1,0:T(8,128)(2,1)S(1)} %get-tuple-element.110), channel_id=1, source_target_pairs={{0,1},{1,0},{2,3},{3,2},{4,5},{5,4},{6,7},{7,6},{8,9},{9,8},{10,11... | collective-permute-start | bytes 786440 | tf_op jit(solution)/shard_map/ppermute | solution.py:466
  238.5 9.2 %collective-permute-start.11 = (bf16[256,512]{1,0:T(8,128)(2,1)S(1)}, bf16[256,512]{1,0:T(8,128)(2,1)S(1)}, u32[]{:S(2)}, u32[]{:S(2)}) collective-permute-start(bf16[256,512]{1,0:T(8,128)(2,1)S(1)} %get-tuple-element.110), channel_id=1, source_target_pairs={{0,16},{8,24},{16,0},{24,8},{1,17},{9,25},{17,1},{25,9},{2,18},{10... | collective-permute-start | bytes 786440 | tf_op jit(solution)/shard_map/ppermute | solution.py:464
  240.0 10.4 %collective-permute-start.12 = (bf16[256,512]{1,0:T(8,128)(2,1)S(1)}, bf16[256,512]{1,0:T(8,128)(2,1)S(1)}, u32[]{:S(2)}, u32[]{:S(2)}) collective-permute-start(bf16[256,512]{1,0:T(8,128)(2,1)S(1)} %get-tuple-element.110), channel_id=1, source_target_pairs={{0,17},{1,16},{2,19},{3,18},{4,21},{5,20},{6,23},{7,22},{8,25},{9,... | collective-permute-start | bytes 786440 | tf_op jit(solution)/shard_map/ppermute | solution.py:470
  250.4 2.7 %collective-permute-start.13 = (bf16[1024,512]{1,0:T(8,128)(2,1)S(1)}, bf16[1024,512]{1,0:T(8,128)(2,1)S(1)}, u32[]{:S(2)}, u32[]{:S(2)}) collective-permute-start(bf16[1024,512]{1,0:T(8,128)(2,1)S(1)} %constant_dynamic-update-slice_fusion.4.own_ref), channel_id=1, source_target_pairs={{0,8},{8,0},{16,24},{24,16},{1,9},{9,1},{17,25},{25,17},{2,10},{10... | collective-permute-start | bytes 3145736 | tf_op jit(solution)/shard_map/ppermute | solution.py:464
  (54 other events, 205.7 us)
where the time goes:
time: 264 us; the launch traced here: 262 us
  waiting for transfers between devices  122 us (46%)
  Pallas kernels  60.7 us (23%)
  local copies, waits for them, and re-layouts  42.5 us (16%)
  starting transfers between devices  35.6 us (13%)
    ppermute x7, waiting for transfers between devices, hop(): lax.ppermute(value, 'narrow', [(i, i ^ narrow_bits) for i in range(narrow)])  43.8 us
    unnamed x119, local copies, waits for them, and re-layouts  42.4 us
    all_to_all x4, waiting for transfers between devices, exchange(): lax.all_to_all(value, 'wide', split_axis=0, concat_axis=0, tiled=True)  41.9 us
    ppermute x8, waiting for transfers between devices, hop(): lax.ppermute(value, 'wide', [(i, i ^ wide_bits) for i in range(wide)])  27.6 us
    all_to_all x4, starting transfers between devices, exchange(): lax.all_to_all(value, 'wide', split_axis=0, concat_axis=0, tiled=True)  18.1 us
    pallas_call x1, Pallas kernels, body(): pl.pallas_call(functools.partial(expert_kernel, experts), grid=(steps,),...  15.1 us
    ppermute x8, starting transfers between devices, hop(): lax.ppermute(value, 'wide', [(i, i ^ wide_bits) for i in range(wide)])  11.5 us
    pallas_call x1, Pallas kernels, body(): pl.pallas_call(functools.partial(backward_kernel, experts), in_specs=[SME...  9.16 us
  transfers between devices with their start and end apart: 21, of which 11 were waited for; matrix products, arithmetic and copies ran while one was open for 0% of the time, Pallas kernels for 14%

commit v1 on v0

--- a/solution.py
+++ b/solution.py
@@ -41,7 +41,50 @@
 
 
 def cost(us):
-    return pl.CostEstimate(flops=int(us * 1.0e9), bytes_accessed=int(us * 1.0e6), transcendentals=0)
+    return pl.CostEstimate(flops=int(us * 1.0e9), bytes_accessed=int(us * 1.0e5), transcendentals=0)
+
+
+class Moved:
+    def __init__(self, value):
+        self.value = value
+        self.shape, self.ndim = value.shape, value.ndim
+
+
+def placed(value):
+    if isinstance(value, Moved):
+        return value.value
+    return value if value.ndim == 1 else pltpu.with_memory_space_constraint(value, pltpu.HBM)
+
+
+def loose(value):
+    return pl.BlockSpec(memory_space=pl.ANY if isinstance(value, Moved) else pltpu.HBM)
+
+
+def whole_spec(dims):
+    return pl.BlockSpec(tuple(dims), lambda *_: (0,) * len(dims))
+
+
+def run(kernel, args, outs, mib, us, name, scratch=(), after=(), grid=(1,), in_specs=None, out_specs=None, free=False, **more):
+    given = len(args)
+    if in_specs is None:
+        in_specs = [SMEM() if a.ndim == 1 else whole_spec(a.shape) for a in args]
+        out_specs = [whole_spec(o.shape) for o in outs]
+
+    def body(*refs):
+        kernel(*refs[:given], *refs[given + len(after) :])
+
+    return pl.pallas_call(
+        body,
+        grid=grid,
+        in_specs=list(in_specs) + [loose(value) for value in after],
+        out_specs=tuple(out_specs),
+        out_shape=tuple(o if free else pltpu.HBM(o.shape, o.dtype) for o in outs),
+        scratch_shapes=list(scratch),
+        compiler_params=params(mib),
+        cost_estimate=cost(us),
+        name=name,
+        **more,
+    )(*map(placed, args), *map(placed, after))
 
 
 def norm_rows(values):
@@ -117,7 +160,6 @@
     out_w_ref,
     gain_two_ref,
     shift_two_ref,
-    spread_ref,
     resid_ref,
     normed_ref,
     query_ref,
@@ -125,7 +167,7 @@
     value_ref,
     weight_ref,
     mixed_ref,
-    sent_ref,
+    second_ref,
 ):
     count, width = tokens_ref.shape
     inputs = tokens_ref[...].astype(F32)
@@ -156,8 +198,11 @@
     resid = inputs + dot(mixed_ref[...], out_w_ref[...])
     resid_ref[...] = resid
     hat, _ = norm_rows(resid)
-    second = (hat * gain_two_ref[...] + shift_two_ref[...]).astype(BF16)
-    sent_ref[...] = dot(spread_ref[...], second).astype(BF16)
+    second_ref[...] = (hat * gain_two_ref[...] + shift_two_ref[...]).astype(BF16)
+
+
+def dispatch_kernel(spread_ref, second_ref, sent_ref):
+    sent_ref[...] = dot(spread_ref[...], second_ref[...]).astype(BF16)
 
 
 def expert_kernel(
@@ -276,7 +321,8 @@
     out_ref[...] = (one_ref[...].astype(F32) + two_ref[...].astype(F32)).astype(BF16)
 
 
-def finish_experts_kernel(core_ref, own_ref, other_ref, up_ref, up_bias_ref, down_ref, down_bias_ref):
+def finish_experts_kernel(core_ref, own_ref, other_ref, *refs):
+    up_ref, up_bias_ref, down_ref, down_bias_ref = refs[-4:]
     half = up_ref.shape[0] // 2
     first = core_ref[0] == 0
     own = own_ref[0].astype(F32)
@@ -429,6 +475,13 @@
         made[away][size:, :] = small
 
 
+def gather_kernel(*refs):
+    arrived, out_ref = refs[:-1], refs[-1]
+    size = arrived[0].shape[0]
+    for at, ref in enumerate(arrived):
+        out_ref[at * size : (at + 1) * size, :] = ref[...]
+
+
 def last_kernel(given, *refs):
     arrived, chunk_ref, small_ref = refs[:given], refs[given], refs[given + 1]
     size = chunk_ref.shape[0]
@@ -510,36 +563,33 @@
         def exchange(value):
             return lax.all_to_all(value, "wide", split_axis=0, concat_axis=0, tiled=True)
 
-        spread, target, counts, grad_sent = pl.pallas_call(
+        spread, target, counts, grad_sent = run(
             functools.partial(route_kernel, capacity, experts),
-            out_shape=(
+            (picks.T, ranks.T, out_grad),
+            (
                 shape((slots_all, count), BF16),
                 shape((count, 8), F32),
                 shape((8, LANES), F32),
                 shape((slots_all, width), BF16),
             ),
-            compiler_params=params(24),
-            cost_estimate=cost(3),
-            name="route",
-        )(picks.T, ranks.T, out_grad)
+            24,
+            3,
+            "route",
+        )
         grad_rows = exchange(grad_sent)
-
-        resid, normed, queries, keys, values, weights, mixed, sent = pl.pallas_call(
+        token_rows = shape((count, width), BF16)
+        resid, normed, queries, keys, values, weights, mixed, second = run(
             attention_kernel,
-            out_shape=(
-                shape((count, width), F32),
-                shape((count, width), BF16),
-                shape((count, width), BF16),
-                shape((count, width), BF16),
-                shape((count, width), BF16),
-                shape((blocks, pairs, 4 * PATCHES, 2 * PATCHES), BF16),
-                shape((count, width), BF16),
-                shape((slots_all, width), BF16),
-            ),
-            compiler_params=params(32),
-            cost_estimate=cost(10),
-            name="attention",
-        )(tokens, gain_one, shift_one, query_w, key_w, value_w, out_w, gain_two, shift_two, spread)
+            (tokens, gain_one, shift_one, query_w, key_w, value_w, out_w, gain_two, shift_two),
+            (shape((count, width), F32),)
+            + (token_rows,) * 4
+            + (shape((blocks, pairs, 4 * PATCHES, 2 * PATCHES), BF16), token_rows, token_rows),
+            40,
+            10,
+            "attention",
+        )
+        rows_shape = shape((slots_all, width), BF16)
+        (sent,) = run(dispatch_kernel, (spread, second), (rows_shape,), 16, 1, "dispatch", after=(Moved(grad_rows),))
         rows = exchange(sent)
 
         whole = pl.BlockSpec((slots_all, width), lambda f: (0, 0))
@@ -550,176 +600,228 @@
         up_bias_spec = pl.BlockSpec((1, tile), lambda f: (0, f))
         down_bias_spec = pl.BlockSpec((1, width), lambda f: (0, 0))
         router_spec = pl.BlockSpec((LANES, width), lambda f: (0, 0))
-        hidden, inner_grad, rows_grad, gated, gate, router_part = pl.pallas_call(
+        payload = 2 * half + 16
+        hidden_shape = shape((slots_all, hidden_width), BF16)
+        hidden, inner_grad, rows_grad, gated, gate, router_part = run(
             functools.partial(expert_kernel, experts),
-            grid=(steps,),
-            in_specs=[SMEM(), whole, whole, up_spec, up_bias_spec, down_spec, down_bias_spec, router_spec],
-            out_specs=(columns, columns, whole, whole, lanes_whole, router_spec),
-            out_shape=(
-                shape((slots_all, hidden_width), BF16),
-                shape((slots_all, hidden_width), BF16),
-                shape((slots_all, width), BF16),
-                shape((slots_all, width), BF16),
-                shape((slots_all, LANES), F32),
-                shape((LANES, width), F32),
+            (
+                wide_at[None].astype(jnp.int32),
+                Moved(rows),
+                Moved(grad_rows),
+                up_w,
+                up_bias,
+                down_w,
+                down_bias,
+                router_t,
             ),
-            scratch_shapes=[
+            (hidden_shape, hidden_shape, rows_shape, rows_shape, shape((slots_all, LANES), F32), shape((LANES, width), F32)),
+            48,
+            10,
+            "experts",
+            (
                 pltpu.VMEM((slots_all, tile), F32),
                 pltpu.VMEM((slots_all, tile), F32),
                 pltpu.VMEM((slots_all, width), F32),
                 pltpu.VMEM((slots_all, LANES), F32),
                 pltpu.VMEM((slots_all, LANES), F32),
-            ],
-            compiler_params=params(40),
-            cost_estimate=cost(10),
-            name="experts",
-        )(wide_at[None].astype(jnp.int32), rows, grad_rows, up_w, up_bias, down_w, down_bias, router_t)
+            ),
+            grid=(steps,),
+            in_specs=(SMEM(), whole, whole, up_spec, up_bias_spec, down_spec, down_bias_spec, router_spec),
+            out_specs=(columns, columns, whole, whole, lanes_whole, router_spec),
+        )
         back = exchange(rows_grad)
 
-        payload = 2 * half + 16
+        halves = 2
+        per_half = steps // halves
+        payload_shape = shape((per_half, payload, width), BF16)
         payload_spec = pl.BlockSpec((1, payload, width), lambda f: (f, 0, 0))
-        keep, send = pl.pallas_call(
-            weight_kernel,
+        expert_sums = []
+        for side in range(halves):
+            some = pl.BlockSpec((slots_all, tile), lambda f, side=side: (0, side * per_half + f))
+            expert_sums.append(
+                run(
+                    weight_kernel,
+                    (core, Moved(rows), gated, hidden, inner_grad),
+                    (payload_shape,) * 2,
+                    40,
+                    0.5,
+                    "expert_weights",
+                    grid=(per_half,),
+                    in_specs=(SMEM(), whole, whole, some, some),
+                    out_specs=(payload_spec,) * 2,
+                    after=[pair[0] for pair in expert_sums],
+                )
+            )
+
+        def add(one, two, after=()):
+            return run(
+                add_kernel,
+                (one, Moved(two)),
+                (payload_shape,),
+                16,
+                1,
+                "add_halves",
+                grid=(per_half,),
+                in_specs=(payload_spec,) * 2,
+                out_specs=(payload_spec,),
+                after=after,
+            )[0]
+
+        sum_one = add(expert_sums[0][0], hop(expert_sums[0][1], 1, 0))
+        two_keep, two_arrived = expert_sums[1][0], hop(expert_sums[1][1], 1, 0)
+        (produced,) = run(
+            produce_kernel,
+            (hidden, down_w, down_bias, gate),
+            (rows_shape,),
+            32,
+            1,
+            "produce",
+            (pltpu.VMEM((slots_all, width), F32),),
             grid=(steps,),
-            in_specs=[SMEM(), whole, whole, columns, columns],
-            out_specs=(payload_spec, payload_spec),
-            out_shape=(shape((steps, payload, width), BF16),) * 2,
-            compiler_params=params(40),
-            cost_estimate=cost(6),
-            name="expert_weights",
-        )(core, rows, gated, hidden, inner_grad)
-        produced = pl.pallas_call(
-            produce_kernel,
-            grid=(steps,),
-            in_specs=[columns, down_spec, down_bias_spec, lanes_whole],
-            out_specs=whole,
-            out_shape=shape((slots_all, width), BF16),
-            scratch_shapes=[pltpu.VMEM((slots_all, width), F32)],
-            compiler_params=params(32),
-            cost_estimate=cost(4),
-            name="produce",
-        )(hidden, down_w, down_bias, gate)
-
-        def add(one, two):
-            return pl.pallas_call(
-                add_kernel,
-                grid=(steps,),
-                in_specs=[payload_spec, payload_spec],
-                out_specs=payload_spec,
-                out_shape=shape((steps, payload, width), BF16),
-                compiler_params=params(16),
-                cost_estimate=cost(2),
-                name="add_halves",
-            )(one, two)
-
-        expert_sum = add(keep, hop(send, 1, 0))
-        bit = 2
-        while bit < narrow:
-            expert_sum = add(expert_sum, hop(expert_sum, bit, 0))
-            bit *= 2
-        up_grad, up_bias_grad, down_grad, down_bias_grad = pl.pallas_call(
-            finish_experts_kernel,
-            grid=(steps,),
-            in_specs=[SMEM(), payload_spec, payload_spec],
-            out_specs=(up_spec, up_bias_spec, down_spec, down_bias_spec),
-            out_shape=(
+            in_specs=(columns, down_spec, down_bias_spec, lanes_whole),
+            out_specs=(whole,),
+            after=(sum_one,),
+        )
+
+        def over_chips(value, bit=2, after=()):
+            while bit < narrow:
+                value = add(value, hop(value, bit, 0), after)
+                bit *= 2
+            return value
+
+        def finish_experts(side, total, arrived, earlier):
+            spec = lambda dims, at: pl.BlockSpec(dims, lambda f: at(side * per_half + f))
+            outs = (
                 shape((width, hidden_width), F32),
                 shape((1, hidden_width), F32),
                 shape((hidden_width, width), F32),
                 shape((1, width), F32),
+            )
+            return run(
+                finish_experts_kernel,
+                (core, total, Moved(arrived), *earlier),
+                outs,
+                24,
+                0.5,
+                "finish_experts",
+                grid=(per_half,),
+                in_specs=[SMEM(), payload_spec, payload_spec] + [pl.BlockSpec(memory_space=pltpu.HBM)] * len(earlier),
+                out_specs=(
+                    spec((width, tile), lambda f: (0, f)),
+                    spec((1, tile), lambda f: (0, f)),
+                    spec((tile, width), lambda f: (f, 0)),
+                    down_bias_spec,
+                ),
+                input_output_aliases={3 + at: at for at in range(len(earlier))},
+            )
+
+        produced_back = exchange(produced)
+
+        tall = 4 * half + extra
+        keep, send, tokens_grad = run(
+            functools.partial(backward_kernel, experts),
+            (
+                core,
+                target,
+                Moved(back),
+                resid,
+                out_grad,
+                gain_two,
+                tokens,
+                gain_one,
+                query_w,
+                key_w,
+                value_w,
+                out_w,
+                normed,
+                queries,
+                keys,
+                values,
+                weights,
+                mixed,
+                counts,
+                router_part,
             ),
-            compiler_params=params(24),
-            cost_estimate=cost(4),
-            name="finish_experts",
-        )(core, expert_sum, hop(expert_sum, 1, 0))
-
-        produced_back = exchange(produced)
-        block_out = pl.pallas_call(
-            combine_kernel,
-            out_shape=shape((count, width), BF16),
-            compiler_params=params(16),
-            cost_estimate=cost(2),
-            name="combine",
-        )(target, produced_back, resid)
-
-        tall = 4 * half + extra
-        keep, send, tokens_grad = pl.pallas_call(
-            functools.partial(backward_kernel, experts),
-            in_specs=[SMEM()] + [VMEM()] * 19,
-            out_shape=(shape((tall, width), BF16), shape((tall, width), BF16), shape((count, width), BF16)),
-            scratch_shapes=[pltpu.VMEM((count, width), BF16)] * 4 + [pltpu.VMEM((count, width), F32)],
-            compiler_params=params(32),
-            cost_estimate=cost(12),
-            name="backward",
-        )(
-            core,
-            target,
-            back,
-            resid,
-            out_grad,
-            gain_two,
-            tokens,
-            gain_one,
-            query_w,
-            key_w,
-            value_w,
-            out_w,
-            normed,
-            queries,
-            keys,
-            values,
-            weights,
-            mixed,
-            counts,
-            router_part,
+            (shape((tall, width), BF16), shape((tall, width), BF16), token_rows),
+            48,
+            2,
+            "backward",
+            [pltpu.VMEM((count, width), BF16)] * 4 + [pltpu.VMEM((count, width), F32)],
+            after=(sum_one, produced, Moved(two_arrived)),
         )
 
-        def share(index, arrived):
+        def share(index, arrived, after=()):
             size = (arrived[0].shape[0] - extra) // 4
-            return pl.pallas_call(
+            return run(
                 functools.partial(share_kernel, len(arrived), 4),
-                in_specs=[SMEM()] + [VMEM()] * len(arrived),
-                out_shape=(shape((size + extra, width), BF16),) * 4,
-                compiler_params=params(16),
-                cost_estimate=cost(1),
-                name="share",
-            )(index, *arrived)
+                (index, arrived[0] if size == half else Moved(arrived[0]), *map(Moved, arrived[1:])),
+                (shape((size + extra, width), BF16),) * 4,
+                16,
+                0.05,
+                "share",
+                after=after,
+                free=True,
+            )
+
+        def last(arrived, after=()):
+            return run(
+                functools.partial(last_kernel, len(arrived)),
+                tuple(map(Moved, arrived)),
+                (shape((half // 4, width), BF16), shape((extra, width), BF16)),
+                16,
+                0.05,
+                "last",
+                after=after,
+                free=True,
+            )
+
+        def gather(arrived, after=()):
+            rows_in = sum(value.shape[0] for value in arrived)
+            return run(
+                gather_kernel,
+                tuple(map(Moved, arrived)),
+                (shape((rows_in, width), BF16),),
+                16,
+                0.05,
+                "gather",
+                after=after,
+                free=True,
+            )[0]
+
+        def spread_out(parts, bits):
+            return [parts[0]] + [hop(part, *bit) for part, bit in zip(parts[1:], bits[1:])]
 
         places = ((0, 0), (0, 1), (2, 0), (2, 1))
         inner_places = ((0, 0), (0, 2), (0, 4), (0, 6))
-        parts = share(place, [keep, hop(send, 1, 0)])
-        parts = [parts[0]] + [hop(part, *bits) for part, bits in zip(parts[1:], places[1:])]
-        parts = share(inner_place, parts)
-        parts = [parts[0]] + [hop(part, *bits) for part, bits in zip(parts[1:], inner_places[1:])]
-
-        def last(arrived):
-            size = half // 4
-            return pl.pallas_call(
-                functools.partial(last_kernel, len(arrived)),
-                out_shape=(shape((size, width), BF16), shape((extra, width), BF16)),
-                compiler_params=params(16),
-                cost_estimate=cost(1),
-                name="last",
-            )(*arrived)
-
-        chunk, small = last(parts)
+        one_arrived = hop(sum_one, 2, 0)
+        parts = share(place, [keep, hop(send, 1, 0)], (Moved(one_arrived),))
+        sum_one = over_chips(add(sum_one, one_arrived, (Moved(parts[0]),)), 4)
+        parts = share(inner_place, spread_out(parts, places), (sum_one,))
+        sum_two = add(two_keep, two_arrived, (Moved(parts[0]),))
+        parts = spread_out(parts, inner_places)
+        (block_out,) = run(combine_kernel, (target, Moved(produced_back), resid), (token_rows,), 16, 0.1, "combine")
+        chunk, small = last(parts, (block_out, sum_two))
         others = [(bit, 0) for bit in (4, 8, 16, 32, 64) if bit < narrow]
         others += [(0, bit) for bit in (8, 16, 32, 64) if bit < wide]
         for bits in others:
             joined = jnp.concatenate([chunk, small], axis=0)
             chunk, small = last([joined, hop(joined, *bits)])
-        chunk = jnp.concatenate([chunk] + [hop(chunk, *bits) for bits in inner_places[1:]], axis=0)
-        chunk = jnp.concatenate([chunk] + [hop(chunk, *bits) for bits in places[1:]], axis=0)
-        outs = pl.pallas_call(
+        finished = finish_experts(0, sum_one, hop(sum_one, 1, 0), ())
+        chunk = gather(spread_out([chunk] * 4, inner_places), finished[:1])
+        sum_two = over_chips(sum_two, after=(Moved(chunk),))
+        finished = finish_experts(1, sum_two, hop(sum_two, 1, 0), finished)
+        chunk = gather(spread_out([chunk] * 4, places), finished[:1])
+        up_grad, up_bias_grad, down_grad, down_bias_grad = finished
+        outs = run(
             functools.partial(finish_shared_kernel, experts),
-            in_specs=[SMEM()] + [VMEM()] * 3,
-            out_shape=(shape((width, width), F32),) * 4
+            (jnp.concatenate([core, place, inner_place]), Moved(chunk), Moved(hop(chunk, 1, 0)), small),
+            (shape((width, width), F32),) * 4
             + (shape((1, width), F32),) * 4
             + (shape((experts, width), F32), shape((2, experts), jnp.int32)),
-            compiler_params=params(24),
-            cost_estimate=cost(3),
-            name="finish_shared",
-        )(jnp.concatenate([core, place, inner_place]), chunk, hop(chunk, 1, 0), small)
+            32,
+            3,
+            "finish_shared",
+        )
         query_grad, key_grad, value_grad, out_w_grad, g_one, s_one, g_two, s_two, router_grad, tallies = outs
         return (
             block_out,

time: 264 us -> 198 us (0.75)
  waiting for transfers between devices: 122 us -> 74.6 us
  local copies, waits for them, and re-layouts: 42.5 us -> 0.67 us
  Pallas kernels: 60.7 us -> 82.1 us
  starting transfers between devices: 35.6 us -> 39 us
    unnamed x119 -> x4, local copies, waits for them, and re-layouts: 42.4 us -> 0.01 us
    ppermute x7 -> x10, waiting for transfers between devices: 43.8 us -> 9.26 us  [hop(): lax.ppermute(value, 'narrow', [(i, i ^ narrow_bits) for i in range(narrow)])]
    pallas_call x14 -> x21, Pallas kernels: 60.7 us -> 82.1 us  [run(): pl.pallas_call(body, grid=grid, in_specs=list(in_specs) + [loose(value) f...]
    ppermute x8, waiting for transfers between devices: 27.6 us -> 21.7 us  [hop(): lax.ppermute(value, 'wide', [(i, i ^ wide_bits) for i in range(wide)])]
    all_to_all x4, waiting for transfers between devices: 41.9 us -> 37.3 us  [exchange(): lax.all_to_all(value, 'wide', split_axis=0, concat_axis=0, tiled=True)]
  transfers between devices with their start and end apart: 21 -> 24, of which waited for: 11 -> 12; matrix products, arithmetic and copies ran while one was open for 0% -> 0% of each run, Pallas kernels for 14% -> 27%
where the time goes in v1:
time: 198 us; the launch traced here: 197 us
  Pallas kernels  82.1 us (41%)
  waiting for transfers between devices  74.6 us (38%)
  starting transfers between devices  39 us (20%)
    pallas_call x21, Pallas kernels, run(): pl.pallas_call(body, grid=grid, in_specs=list(in_specs) + [loose(value) f...  82.1 us
    all_to_all x4, waiting for transfers between devices, exchange(): lax.all_to_all(value, 'wide', split_axis=0, concat_axis=0, tiled=True)  37.3 us
    ppermute x8, waiting for transfers between devices, hop(): lax.ppermute(value, 'wide', [(i, i ^ wide_bits) for i in range(wide)])  21.7 us
    all_to_all x4, starting transfers between devices, exchange(): lax.all_to_all(value, 'wide', split_axis=0, concat_axis=0, tiled=True)  20.5 us
    ppermute x8, starting transfers between devices, hop(): lax.ppermute(value, 'wide', [(i, i ^ wide_bits) for i in range(wide)])  10.9 us
    ppermute x10, waiting for transfers between devices, hop(): lax.ppermute(value, 'narrow', [(i, i ^ narrow_bits) for i in range(narrow)])  9.26 us
    ppermute x2, waiting for transfers between devices, hop(): return lax.ppermute(value, ('narrow', 'wide'), pairs)  6.24 us
    ppermute x10, starting transfers between devices, hop(): lax.ppermute(value, 'narrow', [(i, i ^ narrow_bits) for i in range(narrow)])  4.37 us
  transfers between devices with their start and end apart: 24, of which 12 were waited for; matrix products, arithmetic and copies ran while one was open for 0% of the time, Pallas kernels for 27%

profile of v1, /device:TPU:0, one launch (start us, length us, event | category | flops | bytes accessed | tf_op | source)
XLA Modules:
  0.0 197.2 jit_solution(7170441527381282410)
XLA Ops:
  0.6 3.4 %route.1 = (bf16[832,384]{1,0:T(8,128)(2,1)}, f32[384,8]{1,0:T(8,128)}, f32[8,128]{1,0:T(8,128)}, bf16[832,512]{1,0:T(8,128)(2,1)}) custom-call(s32[2,384]{1,0:T(2,128)} %bitcast.50, s32[2,384]{1,0:T(2,128)} %bitcast.51, bf16[384,512]{1,0:T(8,128)(2,1)} %refs_4_.5), custom_call_target="tpu_custom_call" | custom-call | flops 3000000000 | bytes 300000 | tf_op jit(solution)/shard_map/route/pallas_call | solution.py:76
  4.0 7.3 %all-to-all-start = ((bf16[8,104,512]{2,1,0:T(8,128)(2,1)}), bf16[8,104,512]{2,1,0:T(8,128)(2,1)S(1)}, u32[]{:S(2)}, u32[]{:S(2)}) async-start(bf16[8,104,512]{2,1,0:T(8,128)(2,1)} %bitcast.42), calls=%async_computation | async-start | bytes 1703936 | tf_op jit(solution)/shard_map/all_to_all | solution.py:564
  11.3 5.3 %attention.1 = (f32[384,512]{1,0:T(8,128)}, bf16[384,512]{1,0:T(8,128)(2,1)}, bf16[384,512]{1,0:T(8,128)(2,1)}, bf16[384,512]{1,0:T(8,128)(2,1)}, bf16[384,512]{...) custom-call(bf16[384,512]{1,0:T(8,128)(2,1)} %refs_6_.5, ...), custom_call_target="tpu_custom_call" | custom-call | flops 10000000000 | bytes 1000000 | tf_op jit(solution)/shard_map/attention/pallas_call | solution.py:76
  16.6 16.3 %all-to-all-done = bf16[8,104,512]{2,1,0:T(8,128)(2,1)S(1)} async-done(((bf16[8,104,512]{2,1,0:T(8,128)(2,1)}), bf16[8,104,512]{2,1,0:T(8,128)(2,1)S(1)}, u32[]{:S(2)}, u32[]{:S(2)}) %all-to-all-start) | async-done | bytes 852000 | tf_op jit(solution)/shard_map/all_to_all | solution.py:564
  32.9 2.7 %dispatch.1 = bf16[832,512]{1,0:T(8,128)(2,1)} custom-call(bf16[832,384]{1,0:T(8,128)(2,1)} %get-tuple-element.70.refs_0_, bf16[384,512]{1,0:T(8,128)(2,1)} %get-tuple-element.71.refs_1_, bf16[832,512]{1,0:T(8,128)(2,1)S(1)} %bitcast.34), custom_call_target="tpu_custom_call" | custom-call | flops 1000000000 | bytes 100000 | tf_op jit(solution)/shard_map/dispatch/pallas_call | solution.py:76
  35.6 3.7 %all-to-all-start.1 = ((bf16[8,104,512]{2,1,0:T(8,128)(2,1)}), bf16[8,104,512]{2,1,0:T(8,128)(2,1)S(1)}, u32[]{:S(2)}, u32[]{:S(2)}) async-start(bf16[8,104,512]{2,1,0:T(8,128)(2,1)} %bitcast.43), calls=%async_computation.1 | async-start | bytes 1703936 | tf_op jit(solution)/shard_map/all_to_all | solution.py:564
  40.0 21.0 %all-to-all-done.1 = bf16[8,104,512]{2,1,0:T(8,128)(2,1)S(1)} async-done(((bf16[8,104,512]{2,1,0:T(8,128)(2,1)}), bf16[8,104,512]{2,1,0:T(8,128)(2,1)S(1)}, u32[]{:S(2)}, u32[]{:S(2)}) %all-to-all-start.1) | async-done | bytes 852000 | tf_op jit(solution)/shard_map/all_to_all | solution.py:564
  61.0 16.8 %experts.1 = (bf16[832,2048]{1,0:T(8,128)(2,1)}, bf16[832,2048]{1,0:T(8,128)(2,1)}, bf16[832,512]{1,0:T(8,128)(2,1)}, bf16[832,512]{1,0:T(8,128)(2,1)}, f32[832,128]{1,0:T(8,128)}, /*index=5*/f32[128,512]{1,0:T(8,128)}) custom-call(s32[1]{0:T(128)} %bitcast.2.refs_0_, bf16[832,512]{1,0:T(8,128)(2,1)S(1)} %bitcast.29, bf16[832,512]{1,0:T(8,128)(2,1)S(1)} %bitcast.35, ...), custom_call_target="tpu_custom_call" | custom-call | flops 10000000000 | bytes 1000000 | tf_op jit(solution)/shard_map/experts/pallas_call | solution.py:76
  77.8 3.7 %all-to-all-start.3 = ((bf16[8,104,512]{2,1,0:T(8,128)(2,1)}), bf16[8,104,512]{2,1,0:T(8,128)(2,1)S(1)}, u32[]{:S(2)}, u32[]{:S(2)}) async-start(bf16[8,104,512]{2,1,0:T(8,128)(2,1)} %bitcast.41), calls=%async_computation.3 | async-start | bytes 1703936 | tf_op jit(solution)/shard_map/all_to_all | solution.py:564
  81.6 5.8 %expert_weights.2 = (bf16[2,528,512]{2,1,0:T(8,128)(2,1)}, bf16[2,528,512]{2,1,0:T(8,128)(2,1)}) custom-call(s32[1]{0:T(128)} %bitcast.14.refs_0_, bf16[832,512]{1,0:T(8,128)(2,1)S(1)} %bitcast.30, bf16[832,512]{1,0:T(8,128)(2,1)} %get-tuple-element.75.refs_2_, bf16[832,2048]{1,0:T(8,128)(2,1)} %get-tuple-element.73.refs_3_.refs_0_, ...), custom_call_target="tpu_custom_call" | custom-call | flops 500000000 | bytes 50000 | tf_op jit(solution)/shard_map/expert_weights/pallas_call | solution.py:76
  87.4 5.8 %expert_weights.3 = (bf16[2,528,512]{2,1,0:T(8,128)(2,1)}, bf16[2,528,512]{2,1,0:T(8,128)(2,1)}) custom-call(s32[1]{0:T(128)} %bitcast.14.refs_0_, bf16[832,512]{1,0:T(8,128)(2,1)S(1)} %bitcast.31, bf16[832,512]{1,0:T(8,128)(2,1)} %get-tuple-element.75.refs_2_, bf16[832,2048]{1,0:T(8,128)(2,1)} %get-tuple-element.73.refs_3_.refs_0_, ...), custom_call_target="tpu_custom_call" | custom-call | flops 500000000 | bytes 50000 | tf_op jit(solution)/shard_map/expert_weights/pallas_call | solution.py:76
  97.4 5.8 %produce.1.refs_21_ = bf16[832,512]{1,0:T(8,128)(2,1)} custom-call(bf16[832,2048]{1,0:T(8,128)(2,1)} %get-tuple-element.73.refs_3_.refs_0_, bf16[2048,512]{1,0:T(8,128)(2,1)} %bitcast.40, f32[1,512]{1,0:T(1,128)} %refs_2_.3, f32[832,128]{1,0:T(8,128)} %get-tuple-element.74.refs_3_, bf16[2,528,512]{2,1,0:T(8,128)(2,1)} %add_halves.4.refs_4_.refs_20_.refs_0_), custom_call_target="tpu_custom_call" | custom-call | flops 1000000000 | bytes 100000 | tf_op jit(solution)/shard_map/produce/pallas_call | solution.py:76
  103.3 12.4 %backward.1 = (bf16[1040,512]{1,0:T(8,128)(2,1)}, bf16[1040,512]{1,0:T(8,128)(2,1)}, bf16[384,512]{1,0:T(8,128)(2,1)}) custom-call(s32[1]{0:T(128)} %bitcast.14.refs_0_, f32[384,8]{1,0:T(8,128)} %get-tuple-element.69.refs_0_.refs_1_, bf16[832,512]{1,0:T(8,128)(2,1)S(1)} %bitcast.32, f32[384,512]{1,0:T(8,128)} %get-tuple-element.79.refs_2_.refs_3_, ...), custom_call_target="tpu_custom_call" | custom-call | flops 2000000000 | bytes 200000 | tf_op jit(solution)/shard_map/backward/pallas_call | solution.py:76
  115.7 5.8 %all-to-all-start.2 = ((bf16[8,104,512]{2,1,0:T(8,128)(2,1)}), bf16[8,104,512]{2,1,0:T(8,128)(2,1)S(1)}, u32[]{:S(2)}, u32[]{:S(2)}) async-start(bf16[8,104,512]{2,1,0:T(8,128)(2,1)} %bitcast.37), calls=%async_computation.2 | async-start | bytes 1703936 | tf_op jit(solution)/shard_map/all_to_all | solution.py:564
  130.5 15.1 %collective-permute-done.4.refs_2_ = bf16[272,512]{1,0:T(8,128)(2,1)S(1)} collective-permute-done((bf16[272,512]{1,0:T(8,128)(2,1)}, bf16[272,512]{1,0:T(8,128)(2,1)S(1)}, u32[]{:S(2)}, u32[]{:S(2)}) %collective-permute-start.4) | collective-permute-done | bytes 278560 | tf_op jit(solution)/shard_map/ppermute | solution.py:519
  150.0 2.9 %collective-permute-start.8 = (bf16[80,512]{1,0:T(8,128)(2,1)S(1)}, bf16[80,512]{1,0:T(8,128)(2,1)S(1)}, u32[]{:S(2)}, u32[]{:S(2)}) collective-permute-start(bf16[80,512]{1,0:T(8,128)(2,1)S(1)} %get-tuple-element.99), channel_id=1, source_target_pairs={{0,4},{1,5},{2,6},{3,7},{4,0},{5,1},{6,2},{7,3},{8,12},{9,13},{10,... | collective-permute-start | bytes 245768 | tf_op jit(solution)/shard_map/ppermute | solution.py:519
  152.9 2.6 %combine.1.refs_4_ = bf16[384,512]{1,0:T(8,128)(2,1)} custom-call(f32[384,8]{1,0:T(8,128)} %get-tuple-element.69.refs_0_.refs_1_, bf16[832,512]{1,0:T(8,128)(2,1)S(1)} %bitcast.33, f32[384,512]{1,0:T(8,128)} %get-tuple-element.79.refs_2_.refs_3_), custom_call_target="tpu_custom_call" | custom-call | flops 100000000 | bytes 10000 | tf_op jit(solution)/shard_map/combine/pallas_call | solution.py:76
  163.8 3.4 %finish_experts.2 = (f32[512,2048]{1,0:T(8,128)}, f32[1,2048]{1,0:T(1,128)}, f32[2048,512]{1,0:T(8,128)}, f32[1,512]{1,0:T(1,128)}) custom-call(s32[1]{0:T(128)} %bitcast.14.refs_0_, bf16[2,528,512]{2,1,0:T(8,128)(2,1)} %add_halves.5.refs_5_.refs_1_, bf16[2,528,512]{2,1,0:T(8,128)(2,1)} %collective-permute-done.13.refs_2_), custom_call_target="tpu_custom_call" | custom-call | flops 500000000 | bytes 50000 | tf_op jit(solution)/shard_map/finish_experts/pallas_call | solution.py:76
  168.1 5.6 %collective-permute-done.17.refs_1_ = bf16[2,528,512]{2,1,0:T(8,128)(2,1)S(1)} collective-permute-done((bf16[2,528,512]{2,1,0:T(8,128)(2,1)}, bf16[2,528,512]{2,1,0:T(8,128)(2,1)S(1)}, u32[]{:S(2)}, u32[]{:S(2)}) %collective-permute-start.17) | collective-permute-done | bytes 1081376 | tf_op jit(solution)/shard_map/ppermute | solution.py:517
  176.3 3.0 %collective-permute-start.16 = (bf16[256,512]{1,0:T(8,128)(2,1)S(1)}, bf16[256,512]{1,0:T(8,128)(2,1)S(1)}, u32[]{:S(2)}, u32[]{:S(2)}) collective-permute-start(bf16[256,512]{1,0:T(8,128)(2,1)S(1)} %gather.2.refs_2_.refs_0_), channel_id=1, source_target_pairs={{0,17},{1,16},{2,19},{3,18},{4,21},{5,20},{6,23},{7,22},{8,25},{9,... | collective-permute-start | bytes 786440 | tf_op jit(solution)/shard_map/ppermute | solution.py:523
  179.4 3.2 %finish_experts.3 = (f32[512,2048]{1,0:T(8,128)}, f32[1,2048]{1,0:T(1,128)}, f32[2048,512]{1,0:T(8,128)}, f32[1,512]{1,0:T(1,128)}) custom-call(s32[1]{0:T(128)} %bitcast.14.refs_0_, bf16[2,528,512]{2,1,0:T(8,128)(2,1)} %add_halves.7.refs_1_, ...), custom_call_target="tpu_custom_call", output_to_operand_aliasing={{0}: (3, {}), {1}: (4, {}), {2}: (5, {}), {3}: (6, {})} | custom-call | flops 500000000 | bytes 50000 | tf_op jit(solution)/shard_map/finish_experts/pallas_call | solution.py:76
  185.2 6.2 %collective-permute-done.16.refs_3_ = bf16[256,512]{1,0:T(8,128)(2,1)S(1)} collective-permute-done((bf16[256,512]{1,0:T(8,128)(2,1)S(1)}, bf16[256,512]{1,0:T(8,128)(2,1)S(1)}, u32[]{:S(2)}, u32[]{:S(2)}) %collective-permute-start.16) | collective-permute-done | bytes 262176 | tf_op jit(solution)/shard_map/ppermute | solution.py:523
  191.6 2.6 %collective-permute-done.19.refs_2_ = bf16[1024,512]{1,0:T(8,128)(2,1)S(1)} collective-permute-done((bf16[1024,512]{1,0:T(8,128)(2,1)S(1)}, bf16[1024,512]{1,0:T(8,128)(2,1)S(1)}, u32[]{:S(2)}, u32[]{:S(2)}) %collective-permute-start.19) | collective-permute-done | bytes 1048608 | tf_op jit(solution)/shard_map/ppermute | solution.py:517
  194.2 2.9 %finish_shared.1 = (f32[512,512]{1,0:T(8,128)}, f32[512,512]{1,0:T(8,128)}, f32[512,512]{1,0:T(8,128)}, f32[512,512]{1,0:T(8,128)}, f32[1,512]{1,0:T(1,128)}, /*...) custom-call(s32[3]{0:T(128)S(1)} %pad_add_fusion.refs_0_, ...), custom_call_target="tpu_custom_call" | custom-call | flops 3000000000 | bytes 300000 | tf_op jit(solution)/shard_map/finish_shared/pallas_call | solution.py:76
  (51 shorter events, 32.7 us)
Async XLA Ops:
  4.0 28.9 %all-to-all-start = ((bf16[8,104,512]{2,1,0:T(8,128)(2,1)}), bf16[8,104,512]{2,1,0:T(8,128)(2,1)S(1)}, u32[]{:S(2)}, u32[]{:S(2)}) async-start(bf16[8,104,512]{2,1,0:T(8,128)(2,1)} %bitcast.42), calls=%async_computation | async-start | bytes 1703936 | tf_op jit(solution)/shard_map/all_to_all | solution.py:564
  35.6 25.4 %all-to-all-start.1 = ((bf16[8,104,512]{2,1,0:T(8,128)(2,1)}), bf16[8,104,512]{2,1,0:T(8,128)(2,1)S(1)}, u32[]{:S(2)}, u32[]{:S(2)}) async-start(bf16[8,104,512]{2,1,0:T(8,128)(2,1)} %bitcast.43), calls=%async_computation.1 | async-start | bytes 1703936 | tf_op jit(solution)/shard_map/all_to_all | solution.py:564
  77.8 25.4 %all-to-all-start.3 = ((bf16[8,104,512]{2,1,0:T(8,128)(2,1)}), bf16[8,104,512]{2,1,0:T(8,128)(2,1)S(1)}, u32[]{:S(2)}, u32[]{:S(2)}) async-start(bf16[8,104,512]{2,1,0:T(8,128)(2,1)} %bitcast.41), calls=%async_computation.3 | async-start | bytes 1703936 | tf_op jit(solution)/shard_map/all_to_all | solution.py:564
  87.4 6.3 %collective-permute-start = (bf16[2,528,512]{2,1,0:T(8,128)(2,1)}, bf16[2,528,512]{2,1,0:T(8,128)(2,1)S(1)}, u32[]{:S(2)}, u32[]{:S(2)}) collective-permute-start(bf16[2,528,512]{2,1,0:T(8,128)(2,1)} %get-tuple-element.78), channel_id=1, source_target_pairs={{0,8},{8,0},{16,24},{24,16},{1,9},{9,1},{17,25},{25,17},{2,10},{10... | collective-permute-start | bytes 3244040 | tf_op jit(solution)/shard_map/ppermute | solution.py:517
  93.3 10.0 %collective-permute-start.1 = (bf16[2,528,512]{2,1,0:T(8,128)(2,1)}, bf16[2,528,512]{2,1,0:T(8,128)(2,1)S(1)}, u32[]{:S(2)}, u32[]{:S(2)}) collective-permute-start(bf16[2,528,512]{2,1,0:T(8,128)(2,1)} %get-tuple-element.89), channel_id=1, source_target_pairs={{0,8},{8,0},{16,24},{24,16},{1,9},{9,1},{17,25},{25,17},{2,10},{10... | collective-permute-start | bytes 3244040 | tf_op jit(solution)/shard_map/ppermute | solution.py:517
  95.9 26.1 %collective-permute-start.3 = (bf16[2,528,512]{2,1,0:T(8,128)(2,1)}, bf16[2,528,512]{2,1,0:T(8,128)(2,1)}, u32[]{:S(2)}, u32[]{:S(2)}) collective-permute-start(bf16[2,528,512]{2,1,0:T(8,128)(2,1)} %add_halves.4.refs_4_.refs_20_.refs_0_), channel_id=1, source_target_pairs={{0,16},{8,24},{16,0},{24,8},{1,17},{9,25},{17,1},{25,9},{2,18},{10... | collective-permute-start | bytes 3244040 | tf_op jit(solution)/shard_map/ppermute | solution.py:517
  115.7 6.3 %collective-permute-start.2 = (bf16[1040,512]{1,0:T(8,128)(2,1)}, bf16[1040,512]{1,0:T(8,128)(2,1)}, u32[]{:S(2)}, u32[]{:S(2)}) collective-permute-start(bf16[1040,512]{1,0:T(8,128)(2,1)} %get-tuple-element.92), channel_id=1, source_target_pairs={{0,8},{8,0},{16,24},{24,16},{1,9},{9,1},{17,25},{25,17},{2,10},{10... | collective-permute-start | bytes 3194888 | tf_op jit(solution)/shard_map/ppermute | solution.py:517
  115.7 37.2 %all-to-all-start.2 = ((bf16[8,104,512]{2,1,0:T(8,128)(2,1)}), bf16[8,104,512]{2,1,0:T(8,128)(2,1)S(1)}, u32[]{:S(2)}, u32[]{:S(2)}) async-start(bf16[8,104,512]{2,1,0:T(8,128)(2,1)} %bitcast.37), calls=%async_computation.2 | async-start | bytes 1703936 | tf_op jit(solution)/shard_map/all_to_all | solution.py:564
  124.6 21.1 %collective-permute-start.4 = (bf16[272,512]{1,0:T(8,128)(2,1)}, bf16[272,512]{1,0:T(8,128)(2,1)S(1)}, u32[]{:S(2)}, u32[]{:S(2)}) collective-permute-start(bf16[272,512]{1,0:T(8,128)(2,1)} %get-tuple-element.94), channel_id=1, source_target_pairs={{0,1},{1,0},{2,3},{3,2},{4,5},{5,4},{6,7},{7,6},{8,9},{9,8},{10,11... | collective-permute-start | bytes 835592 | tf_op jit(solution)/shard_map/ppermute | solution.py:519
  126.4 19.2 %collective-permute-start.5 = (bf16[272,512]{1,0:T(8,128)(2,1)}, bf16[272,512]{1,0:T(8,128)(2,1)S(1)}, u32[]{:S(2)}, u32[]{:S(2)}) collective-permute-start(bf16[272,512]{1,0:T(8,128)(2,1)} %get-tuple-element.95), channel_id=1, source_target_pairs={{0,16},{8,24},{16,0},{24,8},{1,17},{9,25},{17,1},{25,9},{2,18},{10... | collective-permute-start | bytes 835592 | tf_op jit(solution)/shard_map/ppermute | solution.py:517
  127.9 17.7 %collective-permute-start.6 = (bf16[272,512]{1,0:T(8,128)(2,1)S(1)}, bf16[272,512]{1,0:T(8,128)(2,1)S(1)}, u32[]{:S(2)}, u32[]{:S(2)}) collective-permute-start(bf16[272,512]{1,0:T(8,128)(2,1)S(1)} %get-tuple-element.96), channel_id=1, source_target_pairs={{0,17},{1,16},{2,19},{3,18},{4,21},{5,20},{6,23},{7,22},{8,25},{9,... | collective-permute-start | bytes 835592 | tf_op jit(solution)/shard_map/ppermute | solution.py:523
  130.5 33.2 %collective-permute-start.13 = (bf16[2,528,512]{2,1,0:T(8,128)(2,1)}, bf16[2,528,512]{2,1,0:T(8,128)(2,1)}, u32[]{:S(2)}, u32[]{:S(2)}) collective-permute-start(bf16[2,528,512]{2,1,0:T(8,128)(2,1)} %add_halves.5.refs_5_.refs_1_), channel_id=1, source_target_pairs={{0,8},{8,0},{16,24},{24,16},{1,9},{9,1},{17,25},{25,17},{2,10},{10... | collective-permute-start | bytes 3244040 | tf_op jit(solution)/shard_map/ppermute | solution.py:517
  148.0 25.7 %collective-permute-start.17 = (bf16[2,528,512]{2,1,0:T(8,128)(2,1)}, bf16[2,528,512]{2,1,0:T(8,128)(2,1)S(1)}, u32[]{:S(2)}, u32[]{:S(2)}) collective-permute-start(bf16[2,528,512]{2,1,0:T(8,128)(2,1)} %add_halves.6.refs_5_.refs_0_), channel_id=1, source_target_pairs={{0,16},{8,24},{16,0},{24,8},{1,17},{9,25},{17,1},{25,9},{2,18},{10... | collective-permute-start | bytes 3244040 | tf_op jit(solution)/shard_map/ppermute | solution.py:517
  148.5 7.1 %collective-permute-start.7 = (bf16[80,512]{1,0:T(8,128)(2,1)S(1)}, bf16[80,512]{1,0:T(8,128)(2,1)S(1)}, u32[]{:S(2)}, u32[]{:S(2)}) collective-permute-start(bf16[80,512]{1,0:T(8,128)(2,1)S(1)} %get-tuple-element.98), channel_id=1, source_target_pairs={{0,2},{1,3},{2,0},{3,1},{4,6},{5,7},{6,4},{7,5},{8,10},{9,11},{10,... | collective-permute-start | bytes 245768 | tf_op jit(solution)/shard_map/ppermute | solution.py:519
  150.0 7.8 %collective-permute-start.8 = (bf16[80,512]{1,0:T(8,128)(2,1)S(1)}, bf16[80,512]{1,0:T(8,128)(2,1)S(1)}, u32[]{:S(2)}, u32[]{:S(2)}) collective-permute-start(bf16[80,512]{1,0:T(8,128)(2,1)S(1)} %get-tuple-element.99), channel_id=1, source_target_pairs={{0,4},{1,5},{2,6},{3,7},{4,0},{5,1},{6,2},{7,3},{8,12},{9,13},{10,... | collective-permute-start | bytes 245768 | tf_op jit(solution)/shard_map/ppermute | solution.py:519
  152.9 6.3 %collective-permute-start.9 = (bf16[80,512]{1,0:T(8,128)(2,1)S(1)}, bf16[80,512]{1,0:T(8,128)(2,1)S(1)}, u32[]{:S(2)}, u32[]{:S(2)}) collective-permute-start(bf16[80,512]{1,0:T(8,128)(2,1)S(1)} %get-tuple-element.100), channel_id=1, source_target_pairs={{0,6},{1,7},{2,4},{3,5},{4,2},{5,3},{6,0},{7,1},{8,14},{9,15},{10,... | collective-permute-start | bytes 245768 | tf_op jit(solution)/shard_map/ppermute | solution.py:519
  159.3 7.8 %collective-permute-start.10 = (bf16[64,512]{1,0:T(8,128)(2,1)S(1)}, bf16[64,512]{1,0:T(8,128)(2,1)S(1)}, u32[]{:S(2)}, u32[]{:S(2)}) collective-permute-start(bf16[64,512]{1,0:T(8,128)(2,1)S(1)} %get-tuple-element.102.refs_0_), channel_id=1, source_target_pairs={{0,2},{1,3},{2,0},{3,1},{4,6},{5,7},{6,4},{7,5},{8,10},{9,11},{10,... | collective-permute-start | bytes 196616 | tf_op jit(solution)/shard_map/ppermute | solution.py:519
  160.2 6.9 %collective-permute-start.11 = (bf16[64,512]{1,0:T(8,128)(2,1)S(1)}, bf16[64,512]{1,0:T(8,128)(2,1)S(1)}, u32[]{:S(2)}, u32[]{:S(2)}) collective-permute-start(bf16[64,512]{1,0:T(8,128)(2,1)S(1)} %get-tuple-element.102.refs_0_), channel_id=1, source_target_pairs={{0,4},{1,5},{2,6},{3,7},{4,0},{5,1},{6,2},{7,3},{8,12},{9,13},{10,... | collective-permute-start | bytes 196616 | tf_op jit(solution)/shard_map/ppermute | solution.py:519
  161.9 6.2 %collective-permute-start.12 = (bf16[64,512]{1,0:T(8,128)(2,1)S(1)}, bf16[64,512]{1,0:T(8,128)(2,1)S(1)}, u32[]{:S(2)}, u32[]{:S(2)}) collective-permute-start(bf16[64,512]{1,0:T(8,128)(2,1)S(1)} %get-tuple-element.102.refs_0_), channel_id=1, source_target_pairs={{0,6},{1,7},{2,4},{3,5},{4,2},{5,3},{6,0},{7,1},{8,14},{9,15},{10,... | collective-permute-start | bytes 196616 | tf_op jit(solution)/shard_map/ppermute | solution.py:519
  175.9 3.5 %collective-permute-start.18 = (bf16[2,528,512]{2,1,0:T(8,128)(2,1)}, bf16[2,528,512]{2,1,0:T(8,128)(2,1)S(1)}, u32[]{:S(2)}, u32[]{:S(2)}) collective-permute-start(bf16[2,528,512]{2,1,0:T(8,128)(2,1)} %add_halves.7.refs_1_), channel_id=1, source_target_pairs={{0,8},{8,0},{16,24},{24,16},{1,9},{9,1},{17,25},{25,17},{2,10},{10... | collective-permute-start | bytes 3244040 | tf_op jit(solution)/shard_map/ppermute | solution.py:517
  175.9 8.7 %collective-permute-start.14 = (bf16[256,512]{1,0:T(8,128)(2,1)S(1)}, bf16[256,512]{1,0:T(8,128)(2,1)S(1)}, u32[]{:S(2)}, u32[]{:S(2)}) collective-permute-start(bf16[256,512]{1,0:T(8,128)(2,1)S(1)} %gather.2.refs_2_.refs_0_), channel_id=1, source_target_pairs={{0,1},{1,0},{2,3},{3,2},{4,5},{5,4},{6,7},{7,6},{8,9},{9,8},{10,11... | collective-permute-start | bytes 786440 | tf_op jit(solution)/shard_map/ppermute | solution.py:519
  176.0 9.1 %collective-permute-start.15 = (bf16[256,512]{1,0:T(8,128)(2,1)S(1)}, bf16[256,512]{1,0:T(8,128)(2,1)S(1)}, u32[]{:S(2)}, u32[]{:S(2)}) collective-permute-start(bf16[256,512]{1,0:T(8,128)(2,1)S(1)} %gather.2.refs_2_.refs_0_), channel_id=1, source_target_pairs={{0,16},{8,24},{16,0},{24,8},{1,17},{9,25},{17,1},{25,9},{2,18},{10... | collective-permute-start | bytes 786440 | tf_op jit(solution)/shard_map/ppermute | solution.py:517
  176.3 15.1 %collective-permute-start.16 = (bf16[256,512]{1,0:T(8,128)(2,1)S(1)}, bf16[256,512]{1,0:T(8,128)(2,1)S(1)}, u32[]{:S(2)}, u32[]{:S(2)}) collective-permute-start(bf16[256,512]{1,0:T(8,128)(2,1)S(1)} %gather.2.refs_2_.refs_0_), channel_id=1, source_target_pairs={{0,17},{1,16},{2,19},{3,18},{4,21},{5,20},{6,23},{7,22},{8,25},{9,... | collective-permute-start | bytes 786440 | tf_op jit(solution)/shard_map/ppermute | solution.py:523
  191.5 2.7 %collective-permute-start.19 = (bf16[1024,512]{1,0:T(8,128)(2,1)S(1)}, bf16[1024,512]{1,0:T(8,128)(2,1)S(1)}, u32[]{:S(2)}, u32[]{:S(2)}) collective-permute-start(bf16[1024,512]{1,0:T(8,128)(2,1)S(1)} %gather.3.refs_1_), channel_id=1, source_target_pairs={{0,8},{8,0},{16,24},{24,16},{1,9},{9,1},{17,25},{25,17},{2,10},{10... | collective-permute-start | bytes 3145736 | tf_op jit(solution)/shard_map/ppermute | solution.py:517
  (2 other events, 11.5 us)
